TPU v7x, 32 devices: a whole 2x2x4 slice. The times are simulated.
32 devices in a mesh: groups: 2 (over y), adapter: 4 (over z), tensor: 2 (over x), sub: 2 (over core).
Axes of the slice: x: 2, y: 2, z: 4, core: 2. Of those that a mesh axis runs over, the one named last changes fastest.
Arguments:
- tokens: bfloat16 [16384, 8192], P(('groups', 'adapter'), ('tensor', 'sub')), parts along dimension 0, may hold values from -6 to 6
- frozen_weight: bfloat16 [8192, 1024], P(('tensor', 'sub'), 'adapter'), may hold values from -0.0625 to 0.0625
- down_tables: bfloat16 [64, 8192, 64], P('adapter', ('tensor', 'sub')), may hold values from -0.0625 to 0.0625
- up_tables: bfloat16 [64, 64, 1024], P('adapter', None, ('tensor', 'sub')), may hold values from -0.75 to 0.75
- cotangent: bfloat16 [16384, 1024], P(('groups', 'adapter'), ('tensor', 'sub')), parts along dimension 0, may hold values from -6 to 6
- block_owner: int32 [128, 1], P(('groups', 'adapter')), parts along dimension 0, may hold values from 0 to 3; in each aligned block of 16 rows (0 to 15, 16 to 31, ...) at most 8 rows name the same one
- block_region: int32 [128], P(('groups', 'adapter')), parts along dimension 0, may hold values from 0 to 15
Outputs:
- projected: bfloat16 [16384, 1024], P(('groups', 'adapter', 'tensor', 'sub')), parts along dimension 0
- grad_down: bfloat16 [128, 8192, 64], P(('groups', 'adapter'), ('tensor', 'sub')), parts along dimension 0
- grad_up: bfloat16 [128, 64, 1024], P(('groups', 'adapter'), None, ('tensor', 'sub')), parts along dimension 0
There are 2 independent parts, one for each index of `groups`. A program takes and returns all parts, laid end to end along the dimension named above; an argument that names none is the same for every part. Nothing has to cross between parts.
Inputs may be any that keep to these rules, and one draw needn't show every extreme that they name: `block_owner`: in each aligned block of 16 entries (the row blocks of one index of adapter) no owner is named more than 8 times, a bound that some block reaches.
All inputs are finite; a program needn't handle non-finite values.
Results may differ from a plain program's by a relative error of at most 0.015.
Values may be sent and summed in bfloat16 or wider, within the bound.
A program may use at most 192 MiB of HBM per device.

v0:
```python
import jax
import jax.numpy as jnp
from jax import lax
from jax.sharding import PartitionSpec as P

BLOCK = 128


adapter_scale = 0.25


def slot_ranks(owner_rows):
    width = owner_rows.shape[-1]
    earlier = jnp.arange(width)[:, None] < jnp.arange(width)[None, :]
    same = owner_rows[..., :, None] == owner_rows[..., None, :]
    return jnp.sum(same & earlier, axis=-2)


def shards(tokens, frozen_weight, down_tables, up_tables, cotangent, block_owner, block_region):
    lane_index = lax.axis_index(("tensor", "sub"))
    owner_count = lax.axis_size("adapter")
    owner_index = lax.axis_index("adapter")
    tok_rows, d_part = tokens.shape
    reg_dev = down_tables.shape[0]
    adapter_rank_width = down_tables.shape[2]
    key_portion = up_tables.shape[2]
    blocks = tok_rows // BLOCK
    slot_limit = max(2, blocks // owner_count * 2)
    my_owner = block_owner[:, 0]
    my_rank = slot_ranks(my_owner)
    all_owner, all_local = (
        lax.all_gather(my_owner, "adapter", axis=0, tiled=True),
        lax.all_gather(block_region, "adapter", axis=0, tiled=True),
    )
    all_owner = all_owner.reshape(owner_count, blocks)
    all_local = all_local.reshape(owner_count, blocks)
    all_rank = slot_ranks(all_owner)
    slot_ids = jnp.arange(slot_limit)
    pick = (
        (my_owner[:, None, None] == jnp.arange(owner_count)[None, :, None])
        & (my_rank[:, None, None] == slot_ids[None, None, :])
    ).astype(jnp.float32)
    select = jnp.sum(
        (
            (all_owner == owner_index)[..., None, None]
            & (all_rank[..., None, None] == slot_ids[:, None])
            & (all_local[..., None, None] == jnp.arange(reg_dev)[None, :])
        ).astype(jnp.float32),
        axis=1,
    )
    down_flat = down_tables.reshape(reg_dev, d_part * adapter_rank_width)
    up_flat = up_tables.reshape(reg_dev, adapter_rank_width * key_portion)
    select_low = select.astype(jnp.bfloat16)
    send_down = jnp.einsum(
        "scl,lx->scx", select_low, down_flat, preferred_element_type=jnp.float32
    ).astype(jnp.bfloat16)
    send_up = jnp.einsum(
        "scl,lx->scx", select_low, up_flat, preferred_element_type=jnp.float32
    ).astype(jnp.bfloat16)
    got_down, got_up = (
        lax.all_to_all(send_down, "adapter", split_axis=0, concat_axis=0, tiled=True),
        lax.all_to_all(send_up, "adapter", split_axis=0, concat_axis=0, tiled=True),
    )
    pick_low = pick.astype(jnp.bfloat16)
    block_down = jnp.einsum(
        "joc,ocx->jx", pick_low, got_down, preferred_element_type=jnp.float32
    ).astype(jnp.bfloat16)
    block_up_weight = jnp.einsum(
        "joc,ocx->jx", pick_low, got_up, preferred_element_type=jnp.float32
    ).astype(jnp.bfloat16)
    block_down = block_down.reshape(blocks, d_part, adapter_rank_width)
    block_up_weight = block_up_weight.reshape(blocks, adapter_rank_width, key_portion)
    frozen_product = jnp.dot(
        tokens,
        lax.all_gather(frozen_weight, "adapter", axis=1, tiled=True),
        preferred_element_type=jnp.float32,
    )
    column_offset = lane_index * key_portion
    tok_blocks = tokens.reshape(blocks, BLOCK, d_part)
    cotangent_blocks = cotangent.reshape(blocks, BLOCK, key_portion)
    down_part = jnp.einsum(
        "nbd,ndr->nbr", tok_blocks, block_down, preferred_element_type=jnp.float32
    )
    up_part = jnp.einsum(
        "ovq,olq->ovl", cotangent_blocks, block_up_weight, preferred_element_type=jnp.float32
    )
    inner_product = lax.psum(
        jnp.concatenate([down_part, up_part], axis=-1).astype(jnp.bfloat16), ("tensor", "sub")
    ).astype(jnp.float32)
    rank_down_weight = inner_product[..., :adapter_rank_width].astype(jnp.bfloat16)
    rank_up_weight = (adapter_scale * inner_product[..., adapter_rank_width:]).astype(jnp.bfloat16)
    adapter_columns = adapter_scale * jnp.einsum(
        "xzm,xms->xzs", rank_down_weight, block_up_weight, preferred_element_type=jnp.float32
    )
    owned_columns = lax.dynamic_slice_in_dim(
        frozen_product, column_offset, key_portion, 1
    ) + adapter_columns.reshape(tok_rows, key_portion)
    frozen_product = lax.dynamic_update_slice_in_dim(
        frozen_product, owned_columns, column_offset, 1
    )
    projected = lax.psum_scatter(
        frozen_product.astype(jnp.bfloat16), ("tensor", "sub"), scatter_dimension=0, tiled=True
    )
    terms_down = jnp.einsum(
        "nbd,nbr->ndr", tok_blocks, rank_up_weight, preferred_element_type=jnp.float32
    ).reshape(blocks, -1)
    up_gradient_terms = (
        adapter_scale
        * jnp.einsum(
            "gdy,gde->gye", rank_down_weight, cotangent_blocks, preferred_element_type=jnp.float32
        )
    ).reshape(blocks, -1)
    back_down = jnp.einsum("joc,jx->ocx", pick, terms_down, precision=lax.Precision.HIGHEST)
    back_up = jnp.einsum("joc,jx->ocx", pick, up_gradient_terms, precision=lax.Precision.HIGHEST)
    got_back_down, got_back_up = (
        lax.all_to_all(
            back_down.astype(jnp.bfloat16), "adapter", split_axis=0, concat_axis=0, tiled=True
        ).astype(back_down.dtype),
        lax.all_to_all(
            back_up.astype(jnp.bfloat16), "adapter", split_axis=0, concat_axis=0, tiled=True
        ).astype(back_up.dtype),
    )
    grad_down = jnp.einsum("scl,scx->lx", select, got_back_down, precision=lax.Precision.HIGHEST)
    grad_up = jnp.einsum("scl,scx->lx", select, got_back_up, precision=lax.Precision.HIGHEST)
    grad_down = grad_down.reshape(reg_dev, d_part, adapter_rank_width).astype(jnp.bfloat16)
    grad_up = grad_up.reshape(reg_dev, adapter_rank_width, key_portion).astype(jnp.bfloat16)
    return (projected, grad_down, grad_up)


def solution(mesh):
    return jax.shard_map(
        shards,
        mesh=mesh,
        in_specs=(
            P(("groups", "adapter"), ("tensor", "sub")),
            P(("tensor", "sub"), "adapter"),
            P("adapter", ("tensor", "sub"), None),
            P("adapter", None, ("tensor", "sub")),
            P(("groups", "adapter"), ("tensor", "sub")),
            P(("groups", "adapter"), None),
            P(("groups", "adapter")),
        ),
        out_specs=(
            P(("groups", "adapter", "tensor", "sub"), None),
            P(("groups", "adapter"), ("tensor", "sub"), None),
            P(("groups", "adapter"), None, ("tensor", "sub")),
        ),
        check_vma=False,
    )
```

profile of v0, /device:TPU:0, one launch (start us, length us, event | category | flops | bytes accessed | tf_op | source)
XLA Modules:
  0.0 609.3 jit_solution(10517368761074550010)
XLA Ops:
  8.0 1.3 dynamic-slice
  11.6 9.9 %all-reduce.2 = (s32[64]{0:T(128)S(1)}, s32[64]{0:T(128)S(1)}) all-reduce(s32[64]{0:T(128)S(1)} %dynamic-update-slice.1, s32[64]{0:T(128)S(1)} %bitcast_dynamic-update-slice_fusion), channel_id=1, replica_groups=mesh['groups'=2,'adapter'=4,'tensor'=2,'sub'=2] {'adapter'}, use_global_device_ids=true, to_apply=%add.1 | all-reduce | flops 128 | bytes 1024
  21.9 1.3 reshape.153
  23.4 1.4 convolution_convert_fusion.3
  24.8 3.5 all-to-all-start.1
  28.3 8.4 %copy.22 = bf16[16,2048,64]{2,1,0:T(8,128)(2,1)} copy(bf16[16,2048,64]{1,2,0:T(8,128)(2,1)} %param.9) | data formatting | bytes 8388608 | tf_op args[2]
  36.7 9.7 %reshape.151 = bf16[16,131072,1]{1,0,2:T(8,128)(2,1)} reshape(bf16[16,2048,64]{2,1,0:T(8,128)(2,1)} %copy.22) | data formatting | bytes 8388608 | tf_op jit(solution)/shard_map/reshape | solution.py:51
  46.4 7.7 %convolution_convert_fusion.1 = bf16[4,8,131072]{2,1,0:T(8,128)(2,1)} fusion(bf16[16,131072,1]{1,0,2:T(8,128)(2,1)} %reshape.151, f32[4,8,16]{2,1,0:T(8,128)S(1)} %convert_reduce_fusion), kind=kOutput, calls=%fused_computation.1 | convolution fusion | flops 138412544 | bytes 12584960 | tf_op jit(solution)/shard_map/scl,lx->scx/dot_general | solution.py:54
  54.1 5.8 all-to-all-start
  61.2 180.0 %all-to-all-done = bf16[4,8,131072]{2,1,0:T(8,128)(2,1)} async-done(((bf16[4,8,131072]{2,1,0:T(8,128)(2,1)}), bf16[4,8,131072]{2,1,0:T(8,128)(2,1)}, u32[]{:S(2)}, u32[]{:S(2)}) %all-to-all-start) | async-done | bytes 8388640 | tf_op jit(solution)/shard_map/all_to_all | solution.py:61
  241.2 6.7 %fusion = bf16[16,131072]{1,0:T(8,128)(2,1)} fusion(bf16[4,8,131072]{2,1,0:T(8,128)(2,1)} %all-to-all-done, pred[16,8]{0,1:T(8,128)(4,1)S(1)} %iota_compare_fusion.3, pred[16,4]{0,1:T(4,128)(4,1)S(1)} %iota_compare_fusion.4), kind=kOutput, calls=%fused_computation.3 | convolution fusion | flops 136316416 | bytes 12583104 | tf_op jit(solution)/shard_map/joc,ocx->jx/dot_general | solution.py:65
  247.9 11.3 %reshape.130 = bf16[16,2048,64]{2,1,0:T(8,128)(2,1)} reshape(bf16[16,131072]{1,0:T(8,128)(2,1)} %fusion) | data formatting | bytes 8388608 | tf_op jit(solution)/shard_map/reshape | solution.py:71
  259.2 8.6 %fusion.3 = bf16[16,128,64]{1,2,0:T(8,128)(2,1)S(1)} fusion(bf16[16,2048,64]{2,1,0:T(8,128)(2,1)} %reshape.130, bf16[16,128,2048]{2,1,0:T(8,128)(2,1)} %bitcast.65), kind=kOutput, calls=%fused_computation.17 | convolution fusion | flops 537001984 | bytes 12845056 | tf_op jit(solution)/shard_map/nbd,ndr->nbr/dot_general | solution.py:81
  269.2 31.9 %all-reduce.5.cloned.1.call-done = bf16[16,128,128]{1,2,0:T(8,128)(2,1)} async-done(((bf16[16,128,128]{1,2,0:T(8,128)(2,1)}), bf16[16,128,128]{1,2,0:T(8,128)(2,1)}) %all-reduce.5.cloned.1.call-update) | async-done | bytes 524304 | tf_op jit(solution)/shard_map/psum | solution.py:87
  301.1 1.3 convolution_multiply_fusion.1
  302.7 1.9 convolution_convert_fusion.2
  304.6 4.8 all-to-all-start.3
  309.4 7.9 %convolution_bitcast_fusion.2 = f32[16,2048,64]{1,2,0:T(8,128)} fusion(bf16[16,128,2048]{2,1,0:T(8,128)(2,1)} %bitcast.66, bf16[16,128,128]{1,2,0:T(8,128)(2,1)S(1)} %copy-done.2), kind=kOutput, calls=%fused_computation.9 | convolution fusion | flops 537264128 | bytes 17039360 | tf_op jit(solution)/shard_map/nbd,nbr->ndr/dot_general | solution.py:104
  317.3 12.2 %copy.24 = f32[16,2048,64]{2,1,0:T(8,128)} copy(f32[16,2048,64]{1,2,0:T(8,128)} %convolution_bitcast_fusion.2) | data formatting | bytes 16777216 | tf_op jit(solution)/shard_map/nbd,nbr->ndr/dot_general | solution.py:104
  329.5 15.4 %reshape.155 = f32[16,131072,1]{1,0,2:T(8,128)} reshape(f32[16,2048,64]{2,1,0:T(8,128)} %copy.24) | data formatting | bytes 16777216 | tf_op jit(solution)/shard_map/reshape | solution.py:106
  344.9 14.0 %convolution_convert_fusion = bf16[4,8,131072]{2,1,0:T(8,128)(2,1)} fusion(f32[16,131072,1]{1,0,2:T(8,128)} %reshape.155, pred[16,8]{0,1:T(8,128)(4,1)S(1)} %iota_compare_fusion.3, pred[16,4]{0,1:T(4,128)(4,1)S(1)} %iota_compare_fusion.4), kind=kOutput, calls=%fused_computation | convolution fusion | flops 809501184 | bytes 16777408 | tf_op jit(solution)/shard_map/joc,jx->ocx/dot_general | solution.py:113
  358.9 2.4 all-to-all-done.3
  361.3 5.6 all-to-all-start.2
  367.2 51.9 %all-gather.3.cloned.1.call-done = bf16[2048,1024]{1,0:T(8,128)(2,1)} async-done(((bf16[2048,256]{1,0:T(8,128)(2,1)}), bf16[2048,1024]{1,0:T(8,128)(2,1)}) %all-gather.3.cloned.1.call-update) | async-done | bytes 4194320 | tf_op jit(solution)/shard_map/all_gather | solution.py:75
  419.1 12.5 %fusion.28 = f32[2048,1024]{1,0:T(8,128)S(1)} fusion(bf16[2048,2048]{1,0:T(8,128)(2,1)} %param.7, bf16[2048,1024]{1,0:T(8,128)(2,1)} %all-gather.3.cloned.1.call-done), kind=kOutput, calls=%fused_computation.54 | convolution fusion | flops 8589934592 | bytes 20971520 | tf_op jit(solution)/shard_map/dot_general | solution.py:73
  432.6 2.6 convert_element_type.63
  435.9 1.0 copy.28
  436.8 115.5 %all-to-all-done.2 = bf16[4,8,131072]{2,1,0:T(8,128)(2,1)} async-done(((bf16[4,8,131072]{2,1,0:T(8,128)(2,1)}), bf16[4,8,131072]{2,1,0:T(8,128)(2,1)}, u32[]{:S(2)}, u32[]{:S(2)}) %all-to-all-start.2) | async-done | bytes 8388640 | tf_op jit(solution)/shard_map/all_to_all | solution.py:116
  552.3 18.9 %dot_general.70 = bf16[2048,64,8,4]{1,0,2,3:T(8,128)(2,1)} reshape(bf16[131072,8,4]{0,1,2:T(8,128)(2,1)} %bitcast.11) | data formatting | bytes 16777216 | tf_op jit(solution)/shard_map/scl,scx->lx/dot_general | solution.py:123
  571.3 19.0 %copy.25 = bf16[2048,64,8,4]{0,2,3,1:T(8,128)(2,1)} copy(bf16[2048,64,8,4]{1,0,2,3:T(8,128)(2,1)} %dot_general.70) | data formatting | bytes 16777216 | tf_op jit(solution)/shard_map/scl,scx->lx/dot_general | solution.py:123
  590.3 6.7 %bitcast_convert_fusion = bf16[16,2048,64]{1,0,2:T(8,128)(2,1)S(1)} fusion(bf16[2048,64,8,4]{0,2,3,1:T(8,128)(2,1)} %copy.25, f32[4,8,16]{2,1,0:T(8,128)S(1)} %convert_reduce_fusion), kind=kOutput, calls=%fused_computation.8 | convolution fusion | flops 807403520 | bytes 12584960 | tf_op jit(solution)/shard_map/scl,scx->lx/dot_general | solution.py:123
  597.0 4.3 copy.27
  (39 shorter events, 7.0 us)
Async XLA Ops:
  8.0 52.7 %copy-start = (bf16[2048,256]{1,0:T(8,128)(2,1)S(1)}, bf16[2048,256]{1,0:T(8,128)(2,1)}, u32[]{:S(2)}) copy-start(bf16[2048,256]{1,0:T(8,128)(2,1)} %param.11) | copy-start | bytes 3145732
  24.8 29.3 %all-to-all-start.1 = ((bf16[4,8,16384]{2,1,0:T(8,128)(2,1)}), bf16[4,8,16384]{2,1,0:T(8,128)(2,1)S(1)}, u32[]{:S(2)}, u32[]{:S(2)}) async-start(bf16[4,8,16384]{2,1,0:T(8,128)(2,1)} %convolution_convert_fusion.3), calls=%async_computation.1 | async-start | bytes 2097152 | tf_op jit(solution)/shard_map/all_to_all | solution.py:62
  54.1 6.0 copy-start.3
  54.1 187.1 %all-to-all-start = ((bf16[4,8,131072]{2,1,0:T(8,128)(2,1)}), bf16[4,8,131072]{2,1,0:T(8,128)(2,1)}, u32[]{:S(2)}, u32[]{:S(2)}) async-start(bf16[4,8,131072]{2,1,0:T(8,128)(2,1)} %convolution_convert_fusion.1), calls=%async_computation | async-start | bytes 16777216 | tf_op jit(solution)/shard_map/all_to_all | solution.py:61
  59.9 241.3 %all-reduce.5.cloned.1.call-start = ((), (), s32[]{:S(2)}) async-start(), calls=%async_computation.6 | async-start | bytes 1048576 | tf_op jit(solution)/shard_map/psum | solution.py:87
  268.7 150.4 %all-gather.3.cloned.1.call-start = ((), (), s32[]{:S(2)}) async-start(), calls=%async_computation.5 | async-start | bytes 5242880 | tf_op jit(solution)/shard_map/all_gather | solution.py:75
  301.1 8.2 %copy-start.2 = (bf16[16,128,128]{1,2,0:T(8,128)(2,1)S(1)}, bf16[16,128,128]{1,2,0:T(8,128)(2,1)}, u32[]{:S(2)}) copy-start(bf16[16,128,128]{1,2,0:T(8,128)(2,1)} %all-reduce.5.cloned.1.call-done) | copy-start | bytes 1572868
  304.6 56.6 %all-to-all-start.3 = ((bf16[4,8,16384]{2,1,0:T(8,128)(2,1)}), bf16[4,8,16384]{2,1,0:T(8,128)(2,1)S(1)}, u32[]{:S(2)}, u32[]{:S(2)}) async-start(bf16[4,8,16384]{2,1,0:T(8,128)(2,1)} %convolution_convert_fusion.2), calls=%async_computation.4 | async-start | bytes 2097152 | tf_op jit(solution)/shard_map/all_to_all | solution.py:119
  361.3 191.1 %all-to-all-start.2 = ((bf16[4,8,131072]{2,1,0:T(8,128)(2,1)}), bf16[4,8,131072]{2,1,0:T(8,128)(2,1)}, u32[]{:S(2)}, u32[]{:S(2)}) async-start(bf16[4,8,131072]{2,1,0:T(8,128)(2,1)} %convolution_convert_fusion), calls=%async_computation.3 | async-start | bytes 16777216 | tf_op jit(solution)/shard_map/all_to_all | solution.py:116
  366.9 234.4 %reduce-scatter.2.cloned.1.call-start = ((), (), s32[]{:S(2)}) async-start(), calls=%async_computation.7 | async-start | bytes 5242880 | tf_op jit(solution)/shard_map/reduce_scatter | solution.py:101
  571.3 30.1 %copy-start.1 = (bf16[2048,256]{1,0:T(8,128)(2,1)S(1)}, bf16[2048,256]{1,0:T(8,128)(2,1)}, u32[]{:S(2)}) copy-start(bf16[2048,256]{1,0:T(8,128)(2,1)} %param.11) | copy-start | bytes 3145732
Sparse Core Ops, SparseCore 0:
  268.8 32.3 all-reduce.4
  435.4 42.5 reduce-scatter.1
Sparse Core Ops, SparseCore 1:
  270.7 148.3 all-gather.2
where the time goes:
time: 616 us; the launch traced here: 609 us
  waiting for transfers between devices  382 us (62%)
  local copies, waits for them, and re-layouts  105 us (17%)
  matrix products  70.7 us (11%)
  starting transfers between devices  20.2 us (3%)
  between operations  16.9 us (3%)
  blocking collectives  9.89 us (2%)
    all_to_all x1, waiting for transfers between devices, shards(): lax.all_to_all(send_down, 'adapter', split_axis=0, concat_axis=0, tiled=T...  180 us
    all_to_all x1, waiting for transfers between devices, shards(): lax.all_to_all(back_down.astype(jnp.bfloat16), 'adapter', split_axis=0, c...  116 us
    all_gather x1, waiting for transfers between devices, shards(): lax.all_gather(frozen_weight, 'adapter', axis=1, tiled=True)  51.9 us
    dot_general x2, local copies, waits for them, and re-layouts, shards(): jnp.einsum('scl,scx->lx', select, got_back_down, precision=lax.Precision....  37.9 us
    psum x1, waiting for transfers between devices, shards(): lax.psum(jnp.concatenate([down_part, up_part], axis=-1).astype(jnp.bfloat...  31.9 us
    unnamed x17, local copies, waits for them, and re-layouts  16.7 us
    reshape x1, local copies, waits for them, and re-layouts, shards(): terms_down = jnp.einsum('nbd,nbr->ndr', tok_blocks, rank_up_weight, prefe...  15.4 us
    dot_general x1, matrix products, shards(): jnp.einsum('joc,jx->ocx', pick, terms_down, precision=lax.Precision.HIGHEST)  14 us
  transfers between devices with their start and end apart: 7, of which 5 were waited for; matrix products, arithmetic and copies ran while one was open for 24% of the time, Pallas kernels for 0%

commit v1 on v0

v1 whole, which is shorter than its diff:
```python
import functools

import jax
import jax.numpy as jnp
from jax import lax
from jax.experimental import pallas as pl
from jax.experimental.pallas import tpu as pltpu
from jax.sharding import PartitionSpec as P

BLOCK = 128


adapter_scale = 0.25

NT = (((1,), (1,)), ((), ()))
NN = (((1,), (0,)), ((), ()))
TN = (((0,), (0,)), ((), ()))


def dot(a, b, dims):
    return lax.dot_general(a, b, dims, preferred_element_type=jnp.float32)


def params():
    return pltpu.CompilerParams(vmem_limit_bytes=40 * 1024 * 1024)


def up_down_parts(region, up_all, cotangent):
    _, rank, cols = up_all.shape
    rows = cotangent.shape[0]

    def kernel(region_ref, up_ref, cot_ref, out_ref):
        out_ref[...] = dot(up_ref[0], cot_ref[...], NT).astype(out_ref.dtype)

    return pl.pallas_call(
        kernel,
        grid_spec=pltpu.PrefetchScalarGridSpec(
            num_scalar_prefetch=1,
            grid=(rows // BLOCK,),
            in_specs=[
                pl.BlockSpec((1, rank, cols), lambda i, r: (r[i], 0, 0)),
                pl.BlockSpec((BLOCK, cols), lambda i, r: (i, 0)),
            ],
            out_specs=pl.BlockSpec((rank, BLOCK), lambda i, r: (0, i)),
        ),
        out_shape=jax.ShapeDtypeStruct((rank, rows), jnp.bfloat16),
        compiler_params=params(),
    )(region, up_all, cotangent)


def summed_terms(order, slot, low, values, scale):
    rank = low.shape[0]
    rows, cols = values.shape
    blocks = rows // BLOCK

    def kernel(order_ref, slot_ref, low_ref, val_ref, out_ref, total):
        i = pl.program_id(0)
        part = dot(low_ref[...], val_ref[...], NN)
        fresh = slot_ref[i] == i

        @pl.when(fresh)
        def _():
            total[...] = part

        @pl.when(jnp.logical_not(fresh))
        def _():
            total[...] += part

        out_ref[0] = (total[...] * scale).astype(out_ref.dtype)

    return pl.pallas_call(
        kernel,
        grid_spec=pltpu.PrefetchScalarGridSpec(
            num_scalar_prefetch=2,
            grid=(blocks,),
            in_specs=[
                pl.BlockSpec((rank, BLOCK), lambda i, o, s: (0, o[i])),
                pl.BlockSpec((BLOCK, cols), lambda i, o, s: (o[i], 0)),
            ],
            out_specs=pl.BlockSpec((1, rank, cols), lambda i, o, s: (s[i], 0, 0)),
            scratch_shapes=[pltpu.VMEM((rank, cols), jnp.float32)],
        ),
        out_shape=jax.ShapeDtypeStruct((blocks, rank, cols), jnp.bfloat16),
        compiler_params=params(),
    )(order, slot, low, values)


def pack(table_at, term_at, kind, tables, terms):
    count = kind.shape[0]
    _, rank, cols = tables.shape

    def kernel(table_ref_at, term_ref_at, kind_ref, table_ref, term_ref, out_ref):
        what = kind_ref[pl.program_id(0)]

        @pl.when(what == 0)
        def _():
            out_ref[...] = table_ref[...]

        @pl.when(what == 1)
        def _():
            out_ref[...] = term_ref[...]

    return pl.pallas_call(
        kernel,
        grid_spec=pltpu.PrefetchScalarGridSpec(
            num_scalar_prefetch=3,
            grid=(count,),
            in_specs=[
                pl.BlockSpec((1, rank, cols), lambda i, a, b, k: (a[i], 0, 0)),
                pl.BlockSpec((1, rank, cols), lambda i, a, b, k: (b[i], 0, 0)),
            ],
            out_specs=pl.BlockSpec((1, rank, cols), lambda i, a, b, k: (i, 0, 0)),
        ),
        out_shape=jax.ShapeDtypeStruct((count, rank, cols), tables.dtype),
        compiler_params=params(),
    )(table_at, term_at, kind, tables, terms)


def inner_parts(got_at, own_at, own, got, tables, tokens):
    _, rank, cols = tables.shape
    rows = tokens.shape[0]

    def kernel(got_ref_at, own_ref_at, own_ref, got_ref, table_ref, tok_ref, out_ref):
        mine = own_ref[pl.program_id(0)] == 1

        @pl.when(mine)
        def _():
            out_ref[...] = dot(table_ref[0], tok_ref[...], NT).astype(out_ref.dtype)

        @pl.when(jnp.logical_not(mine))
        def _():
            out_ref[...] = dot(got_ref[0], tok_ref[...], NT).astype(out_ref.dtype)

    return pl.pallas_call(
        kernel,
        grid_spec=pltpu.PrefetchScalarGridSpec(
            num_scalar_prefetch=3,
            grid=(rows // BLOCK,),
            in_specs=[
                pl.BlockSpec((1, rank, cols), lambda i, g, t, o: (g[i], 0, 0)),
                pl.BlockSpec((1, rank, cols), lambda i, g, t, o: (t[i], 0, 0)),
                pl.BlockSpec((BLOCK, cols), lambda i, g, t, o: (i, 0)),
            ],
            out_specs=pl.BlockSpec((rank, BLOCK), lambda i, g, t, o: (0, i)),
        ),
        out_shape=jax.ShapeDtypeStruct((rank, rows), jnp.bfloat16),
        compiler_params=params(),
    )(got_at, own_at, own, got, tables, tokens)


def owner_sum(got_at, own_at, valid, got, terms, regions):
    consumers = valid.shape[1] - 1
    _, rank, cols = got.shape

    def kernel(got_ref_at, own_ref_at, valid_ref, *refs):
        i = pl.program_id(0)
        out_ref, total = refs[-2], refs[-1]
        total[...] = jnp.zeros_like(total)
        for c in range(consumers + 1):

            @pl.when(valid_ref[i, c] == 1)
            def _(c=c):
                total[...] += refs[c][0].astype(jnp.float32)

        out_ref[0] = total[...].astype(out_ref.dtype)

    def got_map(c, i, g, t, v):
        return (g[i, c], 0, 0)

    return pl.pallas_call(
        kernel,
        grid_spec=pltpu.PrefetchScalarGridSpec(
            num_scalar_prefetch=3,
            grid=(regions,),
            in_specs=[
                pl.BlockSpec((1, rank, cols), functools.partial(got_map, c))
                for c in range(consumers)
            ]
            + [pl.BlockSpec((1, rank, cols), lambda i, g, t, v: (t[i], 0, 0))],
            out_specs=pl.BlockSpec((1, rank, cols), lambda i, g, t, v: (i, 0, 0)),
            scratch_shapes=[pltpu.VMEM((rank, cols), jnp.float32)],
        ),
        out_shape=jax.ShapeDtypeStruct((regions, rank, cols), jnp.bfloat16),
        compiler_params=params(),
    )(got_at, own_at, valid, *([got] * consumers), terms)


def lora_columns(region, low_down, up_all):
    rank, rows = low_down.shape
    cols = up_all.shape[2]

    def kernel(region_ref, low_ref, up_ref, out_ref):
        out_ref[...] = adapter_scale * dot(low_ref[...], up_ref[0], TN)

    return pl.pallas_call(
        kernel,
        grid_spec=pltpu.PrefetchScalarGridSpec(
            num_scalar_prefetch=1,
            grid=(rows // BLOCK,),
            in_specs=[
                pl.BlockSpec((rank, BLOCK), lambda i, r: (0, i)),
                pl.BlockSpec((1, rank, cols), lambda i, r: (r[i], 0, 0)),
            ],
            out_specs=pl.BlockSpec((BLOCK, cols), lambda i, r: (i, 0)),
        ),
        out_shape=jax.ShapeDtypeStruct((rows, cols), jnp.float32),
        compiler_params=params(),
    )(region, low_down, up_all)


def i32(x):
    return x.astype(jnp.int32)


def shards(tokens, frozen_weight, down_tables, up_tables, cotangent, block_owner, block_region):
    lane_index = lax.axis_index(("tensor", "sub"))
    owners = lax.axis_size("adapter")
    me = lax.axis_index("adapter")
    group = lax.axis_index("groups")
    tok_rows, d_part = tokens.shape
    reg_dev, _, rank_width = down_tables.shape
    key_portion = up_tables.shape[2]
    blocks = tok_rows // BLOCK
    slot_limit = max(2, blocks // owners * 2)
    tables = jnp.swapaxes(down_tables, 1, 2)

    region = block_owner[:, 0] * reg_dev + block_region
    named = lax.all_gather(region, ("groups", "adapter"), axis=0, tiled=True)
    named = named.reshape(-1, owners, blocks)
    regions = owners * reg_dev
    present = i32(jnp.any(named[..., None] == jnp.arange(regions), axis=2))
    present = present.reshape(-1, owners, owners, reg_dev)
    counts = jnp.sum(present, axis=-1)
    apart = 1 - jnp.eye(owners, dtype=jnp.int32)
    need = jnp.max((counts + jnp.swapaxes(counts, 1, 2)) * apart)
    here = lax.dynamic_index_in_dim(present, group, 0, False)
    count = lax.dynamic_index_in_dim(counts, group, 0, False)
    before = jnp.arange(reg_dev)[:, None] < jnp.arange(reg_dev)[None, :]
    ranks = jnp.sum(here[..., :, None] * before, axis=-2)
    mine_in = lax.dynamic_index_in_dim(here, me, 0, False)
    mine_of = lax.dynamic_index_in_dim(here, me, 1, False)
    rank_in = lax.dynamic_index_in_dim(ranks, me, 0, False)
    rank_of = lax.dynamic_index_in_dim(ranks, me, 1, False)
    count_in = lax.dynamic_index_in_dim(count, me, 0, False)
    count_of = lax.dynamic_index_in_dim(count, me, 1, False)

    j = jnp.arange(blocks)
    less = region[:, None] < region[None, :]
    tie = (region[:, None] == region[None, :]) & (j[:, None] < j[None, :])
    place = jnp.sum(i32(less | tie), axis=0)
    order = jnp.sum(i32(place[:, None] == j[None, :]) * j[:, None], axis=0)
    first = jnp.sum(i32(less), axis=0)
    slot = jnp.sum(i32(place[:, None] == j[None, :]) * first[:, None], axis=0)
    term_slot = jnp.sum(i32(region[:, None] < jnp.arange(regions)[None, :]), axis=0)
    term_slot = jnp.minimum(term_slot, blocks - 1).reshape(owners, reg_dev)

    up_all = lax.all_gather(up_tables, "adapter", axis=0, tiled=True)
    up_part = up_down_parts(region, up_all, cotangent)
    low_up = lax.psum(up_part, ("tensor", "sub")).astype(jnp.float32)
    low_up = (adapter_scale * low_up).astype(jnp.bfloat16)
    terms = summed_terms(order, slot, low_up, tokens, 1.0)
    weight = lax.all_gather(frozen_weight, "adapter", axis=1, tiled=True)
    frozen_product = jnp.dot(tokens, weight, preferred_element_type=jnp.float32)

    def exchange(slots, tables, terms, tokens):
        s = jnp.arange(slots)
        takes_table = mine_of[:, :, None] * i32(rank_of[:, :, None] == s)
        shifted = rank_in + count_of[:, None]
        takes_term = mine_in[:, :, None] * i32(shifted[:, :, None] == s)
        table_at = jnp.sum(takes_table * jnp.arange(reg_dev)[:, None], axis=1)
        term_at = jnp.sum(takes_term * term_slot[:, :, None], axis=1)
        other = i32(jnp.arange(owners) != me)[:, None]
        kind = jnp.where(
            other * jnp.sum(takes_table, axis=1) > 0,
            0,
            jnp.where(other * jnp.sum(takes_term, axis=1) > 0, 1, 2),
        )
        send = pack(table_at.reshape(-1), term_at.reshape(-1), i32(kind).reshape(-1), tables, terms)
        got = lax.all_to_all(
            send.reshape(owners, slots, rank_width, d_part),
            "adapter", split_axis=0, concat_axis=0, tiled=True,
        ).reshape(owners * slots, rank_width, d_part)
        flat = (jnp.arange(owners)[:, None] * slots + rank_in).reshape(-1)
        own = i32(block_owner[:, 0] == me)
        pick = i32(region[:, None] == jnp.arange(regions))
        got_at = jnp.sum(pick * flat, axis=1) * (1 - own)
        inner = inner_parts(got_at, block_region * own, own, got, tables, tokens)
        remote = mine_of.T * (1 - i32(jnp.arange(owners) == me))
        back_at = (jnp.arange(owners) * slots + count_in)[None, :] + rank_of.T
        own_terms = lax.dynamic_index_in_dim(mine_in, me, 0, False)
        own_slots = lax.dynamic_index_in_dim(term_slot, me, 0, False)
        valid = jnp.concatenate([remote, own_terms[:, None]], axis=1)
        grad = owner_sum(back_at * remote, own_slots * own_terms, valid, got, terms, reg_dev)
        return inner, grad

    full = 2 * slot_limit
    sizes = sorted({-(-full * f // 16) for f in (8, 9, 10, 11, 12, 14, 16)})
    branch = jnp.sum(i32(need > jnp.array(sizes[:-1], jnp.int32)))
    inner, grad_down = lax.switch(
        branch, [functools.partial(exchange, n) for n in sizes], tables, terms, tokens
    )

    low_down = lax.psum(inner, ("tensor", "sub"))
    lora = lora_columns(region, low_down, up_all)
    column_offset = lane_index * key_portion
    owned = lax.dynamic_slice_in_dim(frozen_product, column_offset, key_portion, 1) + lora
    frozen_product = lax.dynamic_update_slice_in_dim(frozen_product, owned, column_offset, 1)
    projected = lax.psum_scatter(
        frozen_product.astype(jnp.bfloat16), ("tensor", "sub"), scatter_dimension=0, tiled=True
    )

    up_terms = summed_terms(order, slot, low_down, cotangent, adapter_scale)
    s = jnp.arange(slot_limit)
    takes = mine_in[:, :, None] * i32(rank_in[:, :, None] == s)
    up_at = jnp.sum(takes * term_slot[:, :, None], axis=1).reshape(-1)
    up_send = jnp.take(up_terms, up_at, axis=0, mode="clip")
    up_got = lax.all_to_all(
        up_send.reshape(owners, slot_limit, rank_width, key_portion),
        "adapter", split_axis=0, concat_axis=0, tiled=True,
    ).reshape(owners * slot_limit, rank_width, key_portion)
    back_at = (jnp.arange(owners) * slot_limit)[None, :] + jnp.minimum(rank_of.T, slot_limit - 1)
    valid = jnp.concatenate([mine_of.T, jnp.zeros((reg_dev, 1), jnp.int32)], axis=1)
    grad_up = owner_sum(
        back_at * mine_of.T, jnp.zeros((reg_dev,), jnp.int32), valid, up_got, up_got, reg_dev
    )
    return (projected, jnp.swapaxes(grad_down, 1, 2), grad_up)


def solution(mesh):
    return jax.shard_map(
        shards,
        mesh=mesh,
        in_specs=(
            P(("groups", "adapter"), ("tensor", "sub")),
            P(("tensor", "sub"), "adapter"),
            P("adapter", ("tensor", "sub"), None),
            P("adapter", None, ("tensor", "sub")),
            P(("groups", "adapter"), ("tensor", "sub")),
            P(("groups", "adapter"), None),
            P(("groups", "adapter")),
        ),
        out_specs=(
            P(("groups", "adapter", "tensor", "sub"), None),
            P(("groups", "adapter"), ("tensor", "sub"), None),
            P(("groups", "adapter"), None, ("tensor", "sub")),
        ),
        check_vma=False,
    )
```

time: 616 us -> 623 us (1.011)
  local copies, waits for them, and re-layouts: 105 us -> 15.2 us
  waiting for transfers between devices: 382 us -> 467 us
  Pallas kernels: 0 us -> 72.7 us
  matrix products: 70.7 us -> 12.5 us
    pallas_call x0 -> x8, Pallas kernels: none -> 72.7 us  [the longest x2 17.8 us: owner_sum(): pl.pallas_call(kernel, grid_spec=pltpu.PrefetchScalarGridSpec(num_scalar_...]
    dot_general x14 -> x1, matrix products: 70.7 us -> 12.5 us  [shards(): frozen_product = jnp.dot(tokens, weight, preferred_element_type=jnp.float32)]
    all_gather x1 -> x2, waiting for transfers between devices: 51.9 us -> 107 us  [the longest x1 75.6 us: shards(): weight = lax.all_gather(frozen_weight, 'adapter', axis=1, tiled=True)]
    dot_general x3 -> x0, local copies, waits for them, and re-layouts: 50.1 us -> none  [the longest x2 37.9 us: shards(): jnp.einsum('scl,scx->lx', select, got_back_down, precision=lax.Precision....]
    reshape x6 -> x2, local copies, waits for them, and re-layouts: 38 us -> 0.17 us  [the longest x1 0.09 us: exchange(): table_at.reshape(-1)]
    psum x1 -> x2, waiting for transfers between devices: 31.9 us -> 59.4 us  [the longest x1 29.9 us: shards(): low_up = lax.psum(up_part, ('tensor', 'sub')).astype(jnp.float32)]
    unnamed x17 -> x28, local copies, waits for them, and re-layouts: 16.7 us -> 7.33 us
    all_to_all x4 -> x2, starting transfers between devices: 19.7 us -> 15.1 us  [the longest x1 11.5 us: exchange(): lax.all_to_all(send.reshape(owners, slots, rank_width, d_part), 'adapter'...]
  transfers between devices with their start and end apart: 7 -> 7, of which waited for: 5 -> 7; matrix products, arithmetic and copies ran while one was open for 24% -> 1% of each run, Pallas kernels for 0% -> 2%
where the time goes in v1:
time: 623 us; the launch traced here: 621 us
  waiting for transfers between devices  467 us (75%)
  Pallas kernels  72.7 us (12%)
  starting transfers between devices  15.3 us (2%)
  between operations  15.3 us (2%)
  local copies, waits for them, and re-layouts  15.2 us (2%)
  blocking collectives  13 us (2%)
  matrix products  12.5 us (2%)
  other arithmetic  9.65 us (2%)
    all_to_all x1, waiting for transfers between devices, exchange(): lax.all_to_all(send.reshape(owners, slots, rank_width, d_part), 'adapter'...  272 us
    all_gather x1, waiting for transfers between devices, shards(): weight = lax.all_gather(frozen_weight, 'adapter', axis=1, tiled=True)  75.6 us
    all_gather x1, waiting for transfers between devices, shards(): up_all = lax.all_gather(up_tables, 'adapter', axis=0, tiled=True)  31 us
    psum x1, waiting for transfers between devices, shards(): low_up = lax.psum(up_part, ('tensor', 'sub')).astype(jnp.float32)  29.9 us
    psum x1, waiting for transfers between devices, shards(): low_down = lax.psum(inner, ('tensor', 'sub'))  29.5 us
    all_to_all x1, waiting for transfers between devices, shards(): lax.all_to_all(up_send.reshape(owners, slot_limit, rank_width, key_portio...  25.9 us
    pallas_call x2, Pallas kernels, owner_sum(): pl.pallas_call(kernel, grid_spec=pltpu.PrefetchScalarGridSpec(num_scalar_...  17.8 us
    pallas_call x2, Pallas kernels, summed_terms(): pl.pallas_call(kernel, grid_spec=pltpu.PrefetchScalarGridSpec(num_scalar_...  16.6 us
  transfers between devices with their start and end apart: 7, of which 7 were waited for; matrix products, arithmetic and copies ran while one was open for 1% of the time, Pallas kernels for 2%

profile of v1, /device:TPU:0, one launch (start us, length us, event | category | flops | bytes accessed | tf_op | source)
XLA Modules:
  0.0 621.3 jit_solution(17520387731322747927)
XLA Ops:
  8.0 1.2 dynamic-slice.8
  9.9 0.8 fusion.46
  10.6 13.0 %all-reduce.1 = s32[128]{0:T(128)S(1)} all-reduce(s32[128]{0:T(128)S(1)} %get-tuple-element.907), channel_id=1, replica_groups=mesh['groups'=2,'adapter'=4,'tensor'=2,'sub'=2] {'groups','adapter'}, use_global_device_ids=true, to_apply=%add.1 | all-reduce | flops 128 | bytes 1024
  25.1 1.9 fusion.44
  27.2 31.0 %all-gather.5.cloned.1.call-done.up_ref = bf16[64,64,256]{2,1,0:T(8,128)(2,1)} async-done(((bf16[16,64,256]{2,1,0:T(8,128)(2,1)}), bf16[64,64,256]{2,1,0:T(8,128)(2,1)}) %all-gather.5.cloned.1.call-update) | async-done | bytes 2097168 | tf_op jit(solution)/shard_map/all_gather | solution.py:257
  58.2 1.6 copy-done.5
  59.8 1.2 copy-done.7
  61.1 6.8 %shard_map.103 = bf16[64,2048]{1,0:T(8,128)(2,1)} custom-call(s32[16]{0:T(128)S(1)} %get-tuple-element.908.region_ref, bf16[64,64,256]{2,1,0:T(8,128)(2,1)S(1)} %copy-done.5, bf16[2048,256]{1,0:T(8,128)(2,1)S(1)} %copy-done.7), custom_call_target="tpu_custom_call" | custom-call | tf_op jit(solution)/shard_map/pallas_call | solution.py:35
  69.0 29.9 %all-reduce.5.cloned.1.call-done = bf16[64,2048]{1,0:T(8,128)(2,1)} async-done(((bf16[64,2048]{1,0:T(8,128)(2,1)}), bf16[64,2048]{1,0:T(8,128)(2,1)}) %all-reduce.5.cloned.1.call-update) | async-done | bytes 262160 | tf_op jit(solution)/shard_map/psum | solution.py:259
  98.9 1.0 multiply_convert_fusion.low_ref
  99.9 13.4 %shard_map.104 = bf16[16,64,2048]{2,1,0:T(8,128)(2,1)} custom-call(s32[16]{0:T(128)S(1)} %get-tuple-element.876.order_ref, s32[16]{0:T(128)S(1)} %get-tuple-element.875.slot_ref, bf16[64,2048]{1,0:T(8,128)(2,1)S(1)} %multiply_convert_fusion.low_ref, bf16[2048,2048]{1,0:T(8,128)(2,1)} %val_ref.2), custom_call_target="tpu_custom_call" | custom-call | tf_op jit(solution)/shard_map/pallas_call | solution.py:71
  113.3 330.1 %conditional.1 = (bf16[64,2048]{1,0:T(8,128)(2,1)S(1)}, bf16[16,64,2048]{2,1,0:T(8,128)(2,1)}) conditional(s32[]{:T(128)} %clamp.31, (s32[16]{0:T(128)S(1)}, s32[4,16]{1,0:T(4,128)S(1)}, s32[]{:T(128)}, s32[16,1]{0,1:T(1,128)S(1)}, s32[16]{0:T(128)S(1)}, /*index=5*/s32[4,16]{1,0:T(4,128)S(1)}, s32[4,16]{1,0:T(4,128)S(1)}, ...), branch_computations={%region_11.17_spmd, %region_17.23_spmd, %region_23.29_spmd, %regio... | conditional | flops 13955 | bytes 104868464 | solution.py:299
  113.5 0.9 select_reduce_fusion.12
  114.9 14.8 %branch_4_fun.3 = bf16[48,64,2048]{2,1,0:T(8,128)(2,1)S(1)} custom-call(s32[48]{0:T(128)S(1)} %reshape.466.table_ref_at, s32[48]{0:T(128)S(1)} %reshape.467.term_ref_at, s32[48]{0:T(128)S(1)} %select_n.138.kind_ref, bf16[16,64,2048]{2,1,0:T(8,128)(2,1)} %get-tuple-element.280.table_ref, bf16[16,64,2048]{2,1,0:T(8,128)(2,1)} %get-tuple-element.281.term_ref.refs_4_), custom_call_target="tpu_custom_call" | custom-call | tf_op jit(solution)/shard_map/cond/branch_4_fun/pallas_call | solution.py:103
  129.8 4.5 copy-done
  134.2 11.5 %all-to-all-start.4 = ((bf16[4,12,64,2048]{3,2,1,0:T(8,128)(2,1)}), bf16[4,12,64,2048]{3,2,1,0:T(8,128)(2,1)}, u32[]{:S(2)}, u32[]{:S(2)}) async-start(bf16[4,12,64,2048]{3,2,1,0:T(8,128)(2,1)} %bitcast.135), calls=%async_computation.4 | async-start | bytes 25165824 | tf_op jit(solution)/shard_map/cond/branch_4_fun/all_to_all | solution.py:279
  146.4 272.2 %all-to-all-done.4 = bf16[4,12,64,2048]{3,2,1,0:T(8,128)(2,1)} async-done(((bf16[4,12,64,2048]{3,2,1,0:T(8,128)(2,1)}), bf16[4,12,64,2048]{3,2,1,0:T(8,128)(2,1)}, u32[]{:S(2)}, u32[]{:S(2)}) %all-to-all-start.4) | async-done | bytes 12582944 | tf_op jit(solution)/shard_map/cond/branch_4_fun/all_to_all | solution.py:279
  418.6 11.7 %branch_4_fun.5 = bf16[16,64,2048]{2,1,0:T(8,128)(2,1)} custom-call(s32[16,4]{1,0:T(8,128)S(1)} %get-tuple-element.895.got_ref_at, s32[16]{0:T(128)S(1)} %get-tuple-element.946.own_ref_at, s32[16,5]{1,0:T(8,128)S(1)} %pad_add_fusion.4.valid_ref, bf16[48,64,2048]{2,1,0:T(8,128)(2,1)} %bitcast.30.got_ref.refs_0_.refs_1_.refs_2_.refs_3_, ...), custom_call_target="tpu_custom_call" | custom-call | tf_op jit(solution)/shard_map/cond/branch_4_fun/pallas_call | solution.py:170
  430.3 12.8 %branch_4_fun.4 = bf16[64,2048]{1,0:T(8,128)(2,1)S(1)} custom-call(s32[16]{0:T(128)S(1)} %get-tuple-element.897.got_ref_at, s32[16]{0:T(128)S(1)} %get-tuple-element.949.own_ref_at, s32[16]{0:T(128)S(1)} %get-tuple-element.898.own_ref, bf16[48,64,2048]{2,1,0:T(8,128)(2,1)} %bitcast.30.got_ref.refs_0_.refs_1_.refs_2_.refs_3_, ...), custom_call_target="tpu_custom_call" | custom-call | tf_op jit(solution)/shard_map/cond/branch_4_fun/pallas_call | solution.py:134
  444.7 29.5 %all-reduce.7.cloned.1.call-done.low_ref = bf16[64,2048]{1,0:T(8,128)(2,1)} async-done(((bf16[64,2048]{1,0:T(8,128)(2,1)}), bf16[64,2048]{1,0:T(8,128)(2,1)}) %all-reduce.7.cloned.1.call-update) | async-done | bytes 262160 | tf_op jit(solution)/shard_map/psum | solution.py:303
  474.2 1.6 copy-done.6
  475.8 0.9 copy-done.9
  476.7 3.8 shard_map.105
  480.6 75.6 %all-gather.3.cloned.1.call-done = bf16[2048,1024]{1,0:T(8,128)(2,1)} async-done(((bf16[2048,256]{1,0:T(8,128)(2,1)}), bf16[2048,1024]{1,0:T(8,128)(2,1)}) %all-gather.3.cloned.1.call-update) | async-done | bytes 4194320 | tf_op jit(solution)/shard_map/all_gather | solution.py:262
  556.2 12.5 %fusion.47 = f32[2048,1024]{1,0:T(8,128)S(1)} fusion(bf16[2048,2048]{1,0:T(8,128)(2,1)} %val_ref.2, bf16[2048,1024]{1,0:T(8,128)(2,1)} %all-gather.3.cloned.1.call-done), kind=kOutput, calls=%fused_computation.247 | convolution fusion | flops 8589934592 | bytes 20971520 | tf_op jit(solution)/shard_map/dot_general | solution.py:263
  569.3 2.6 convert_element_type.195
  572.2 3.2 shard_map.106
  575.4 1.6 gather_fusion
  577.0 3.5 all-to-all-start.7
  580.8 25.9 %all-to-all-done.7 = bf16[4,8,64,256]{3,2,1,0:T(8,128)(2,1)S(1)} async-done(((bf16[4,8,64,256]{3,2,1,0:T(8,128)(2,1)}), bf16[4,8,64,256]{3,2,1,0:T(8,128)(2,1)S(1)}, u32[]{:S(2)}, u32[]{:S(2)}) %all-to-all-start.7) | async-done | bytes 1048608 | tf_op jit(solution)/shard_map/all_to_all | solution.py:317
  606.7 6.1 shard_map.107
  612.8 2.0 reduce-scatter.2.cloned.1.call-done
  (89 shorter events, 6.5 us)
Async XLA Ops:
  7.2 51.1 %all-gather.5.cloned.1.call-start = ((), (), s32[]{:S(2)}) async-start(), calls=%async_computation.10 | async-start | bytes 2621440 | tf_op jit(solution)/shard_map/all_gather | solution.py:257
  7.9 91.0 %all-reduce.5.cloned.1.call-start = ((), (), s32[]{:S(2)}) async-start(), calls=%async_computation.11 | async-start | bytes 524288 | tf_op jit(solution)/shard_map/psum | solution.py:259
  58.2 1.6 copy-start.5
  59.8 1.2 copy-start.7
  61.1 52.2 %copy-start.23 = (s32[16]{0:T(128)S(1)}, s32[16]{0:T(128)}, u32[]{:S(2)}) copy-start(s32[16]{0:T(128)} %param.21) | copy-start | bytes 196
  61.1 52.2 %copy-start.24 = (s32[16,1]{0,1:T(1,128)S(1)}, s32[16,1]{0,1:T(1,128)}, u32[]{:S(2)}) copy-start(s32[16,1]{0,1:T(1,128)} %param.20) | copy-start | bytes 196
  67.9 406.3 %all-reduce.7.cloned.1.call-start = ((), (), s32[]{:S(2)}) async-start(), calls=%async_computation.12 | async-start | bytes 524288 | tf_op jit(solution)/shard_map/psum | solution.py:303
  69.0 44.3 %copy-start.11 = (s32[16]{0:T(128)}, s32[16]{0:T(128)S(1)}, u32[]{:S(2)}) copy-start(s32[16]{0:T(128)S(1)} %get-tuple-element.875.slot_ref) | copy-start | bytes 196
  69.0 44.3 %copy-start.13 = (s32[16]{0:T(128)}, s32[16]{0:T(128)S(1)}, u32[]{:S(2)}) copy-start(s32[16]{0:T(128)S(1)} %get-tuple-element.876.order_ref) | copy-start | bytes 196
  129.8 4.5 copy-start
  134.2 284.4 %all-to-all-start.4 = ((bf16[4,12,64,2048]{3,2,1,0:T(8,128)(2,1)}), bf16[4,12,64,2048]{3,2,1,0:T(8,128)(2,1)}, u32[]{:S(2)}, u32[]{:S(2)}) async-start(bf16[4,12,64,2048]{3,2,1,0:T(8,128)(2,1)} %bitcast.135), calls=%async_computation.4 | async-start | bytes 25165824 | tf_op jit(solution)/shard_map/cond/branch_4_fun/all_to_all | solution.py:279
  418.6 11.8 %copy-start.19 = (bf16[16,64,2048]{2,1,0:T(8,128)(2,1)S(1)}, bf16[16,64,2048]{2,1,0:T(8,128)(2,1)}, u32[]{:S(2)}) copy-start(bf16[16,64,2048]{2,1,0:T(8,128)(2,1)} %get-tuple-element.280.table_ref) | copy-start | bytes 12582916 | tf_op jit(solution)/shard_map/cond
  443.4 0.7 copy-start.22
  444.1 112.1 %all-gather.3.cloned.1.call-start = ((), (), s32[]{:S(2)}) async-start(), calls=%async_computation.9 | async-start | bytes 5242880 | tf_op jit(solution)/shard_map/all_gather | solution.py:262
  444.7 170.1 %reduce-scatter.2.cloned.1.call-start = ((), (), s32[]{:S(2)}) async-start(), calls=%async_computation.13 | async-start | bytes 5242880 | tf_op jit(solution)/shard_map/reduce_scatter | solution.py:308
  474.2 1.6 copy-start.6
  475.8 0.9 copy-start.9
  569.2 2.9 copy-start.8
  569.2 2.9 copy-start.10
  569.3 2.9 copy-start.12
  569.3 2.9 copy-start.14
  577.0 29.7 %all-to-all-start.7 = ((bf16[4,8,64,256]{3,2,1,0:T(8,128)(2,1)}), bf16[4,8,64,256]{3,2,1,0:T(8,128)(2,1)S(1)}, u32[]{:S(2)}, u32[]{:S(2)}) async-start(bf16[4,8,64,256]{3,2,1,0:T(8,128)(2,1)} %bitcast.62), calls=%async_computation.8 | async-start | bytes 2097152 | tf_op jit(solution)/shard_map/all_to_all | solution.py:317
Sparse Core Ops, SparseCore 0:
  9.6 48.6 all-gather.4
  68.0 30.8 all-reduce.4
  444.2 29.9 all-reduce.6
  475.6 80.5 all-gather.2
  572.0 42.7 reduce-scatter.1

commit v2 on v1

--- a/solution.py
+++ b/solution.py
@@ -185,27 +185,141 @@
     )(got_at, own_at, valid, *([got] * consumers), terms)
 
 
-def lora_columns(region, low_down, up_all):
-    rank, rows = low_down.shape
-    cols = up_all.shape[2]
-
-    def kernel(region_ref, low_ref, up_ref, out_ref):
-        out_ref[...] = adapter_scale * dot(low_ref[...], up_ref[0], TN)
+def line_exchange(count, step_id, send, mask):
+    total, rows, cols = send.shape
+    lag, deep = 2, 3
+
+    def kernel(send_ref, mask_ref, got_ref, own_buf, pass_buf, out_buf, load_sem, pass_sem, send_sem, recv_sem):
+        me = lax.axis_index("adapter")
+        last = lax.axis_size("adapter") - 1
+        barrier = pltpu.get_barrier_semaphore()
+
+        @pl.when(me > 0)
+        def _():
+            pl.semaphore_signal(barrier, inc=1, device_id={"adapter": me - 1}, device_id_type=pl.DeviceIdType.MESH)
+
+        @pl.when(me < last)
+        def _():
+            pl.semaphore_signal(barrier, inc=1, device_id={"adapter": me + 1}, device_id_type=pl.DeviceIdType.MESH)
+
+        inside = (me > 0) & (me < last)
+
+        @pl.when(inside)
+        def _():
+            pl.semaphore_wait(barrier, 2)
+
+        @pl.when(jnp.logical_not(inside))
+        def _():
+            pl.semaphore_wait(barrier, 1)
+
+        def remote(way, t):
+            peer = me + 1 if way == 0 else me - 1
+            slot = lax.rem(t, deep)
+            return pltpu.make_async_remote_copy(
+                src_ref=out_buf.at[way, slot],
+                dst_ref=got_ref.at[way * count + t],
+                send_sem=send_sem.at[way, slot],
+                recv_sem=recv_sem.at[way, t],
+                device_id={"adapter": peer},
+                device_id_type=pl.DeviceIdType.MESH,
+            )
+
+        def own_load(way, t):
+            return pltpu.make_async_copy(send_ref.at[way * count + t], own_buf.at[way], load_sem.at[way])
+
+        def pass_load(way, t):
+            return pltpu.make_async_copy(got_ref.at[way * count + t], pass_buf.at[way], pass_sem.at[way])
+
+        places = (me, last - me)
+
+        def step(i, carry):
+            at = [i - lag * place for place in places]
+            live = [(t >= 0) & (t < count) for t in at]
+            sends = [ok & (place < last) for ok, place in zip(live, places)]
+            for way in (0, 1):
+
+                @pl.when(sends[way])
+                def _(way=way):
+                    own_load(way, at[way]).start()
+
+            for way in (0, 1):
+
+                @pl.when(live[way] & (places[way] > 0))
+                def _(way=way):
+                    remote(way, at[way]).wait_recv()
+
+                @pl.when(sends[way] & (places[way] > 0))
+                def _(way=way):
+                    pass_load(way, at[way]).start()
+
+            for way in (0, 1):
+
+                @pl.when(sends[way])
+                def _(way=way):
+                    t = at[way]
+                    slot = lax.rem(t, deep)
+
+                    @pl.when(t >= deep)
+                    def _():
+                        remote(way, t).wait_send()
+
+                    own_load(way, t).wait()
+
+                    @pl.when(places[way] == 0)
+                    def _():
+                        out_buf[way, slot] = own_buf[way]
+
+                    @pl.when(places[way] > 0)
+                    def _():
+                        pass_load(way, t).wait()
+                        mine = jnp.broadcast_to(mask_ref[way * count + t], (rows, cols)) > 0
+                        out_buf[way, slot] = jnp.where(
+                            mine, own_buf[way].astype(jnp.float32), pass_buf[way].astype(jnp.float32)
+                        ).astype(out_buf.dtype)
+
+                    remote(way, t).start()
+
+            return carry
+
+        lax.fori_loop(0, count + lag * last, step, 0)
+        for way in (0, 1):
+            for t in range(count - deep, count):
+
+                @pl.when(places[way] < last)
+                def _(way=way, t=t):
+                    remote(way, t).wait_send()
 
     return pl.pallas_call(
         kernel,
-        grid_spec=pltpu.PrefetchScalarGridSpec(
-            num_scalar_prefetch=1,
-            grid=(rows // BLOCK,),
-            in_specs=[
-                pl.BlockSpec((rank, BLOCK), lambda i, r: (0, i)),
-                pl.BlockSpec((1, rank, cols), lambda i, r: (r[i], 0, 0)),
-            ],
-            out_specs=pl.BlockSpec((BLOCK, cols), lambda i, r: (i, 0)),
-        ),
-        out_shape=jax.ShapeDtypeStruct((rows, cols), jnp.float32),
-        compiler_params=params(),
-    )(region, low_down, up_all)
+        in_specs=[
+            pl.BlockSpec(memory_space=pl.ANY),
+            pl.BlockSpec(memory_space=pltpu.SMEM),
+        ],
+        out_specs=pl.BlockSpec(memory_space=pl.ANY),
+        out_shape=jax.ShapeDtypeStruct((total, rows, cols), send.dtype),
+        scratch_shapes=[
+            pltpu.VMEM((2, rows, cols), send.dtype),
+            pltpu.VMEM((2, rows, cols), send.dtype),
+            pltpu.VMEM((2, deep, rows, cols), send.dtype),
+            pltpu.SemaphoreType.DMA((2,)),
+            pltpu.SemaphoreType.DMA((2,)),
+            pltpu.SemaphoreType.DMA((2, deep)),
+            pltpu.SemaphoreType.DMA((2, count)),
+        ],
+        compiler_params=pltpu.CompilerParams(
+            collective_id=step_id, has_side_effects=True, vmem_limit_bytes=40 * 1024 * 1024
+        ),
+    )(send, mask)
+
+
+def from_owners(x, owners):
+    if owners > 4:
+        return [y for y in lax.all_gather(x, "adapter", axis=0)], jnp.arange(owners)
+    parts = [x]
+    for shift in range(1, owners):
+        ring = [(i, (i + shift) % owners) for i in range(owners)]
+        parts.append(lax.ppermute(x, "adapter", ring))
+    return parts, lax.rem(lax.axis_index("adapter") - jnp.arange(owners) + owners, owners)
 
 
 def i32(x):
@@ -254,13 +368,77 @@
     term_slot = jnp.sum(i32(region[:, None] < jnp.arange(regions)[None, :]), axis=0)
     term_slot = jnp.minimum(term_slot, blocks - 1).reshape(owners, reg_dev)
 
-    up_all = lax.all_gather(up_tables, "adapter", axis=0, tiled=True)
-    up_part = up_down_parts(region, up_all, cotangent)
+    up_parts, up_place = from_owners(up_tables, owners)
+    up_all = jnp.concatenate(up_parts, axis=0)
+    up_at = jnp.sum(i32(block_owner == jnp.arange(owners)) * up_place, axis=1) * reg_dev + block_region
+    up_part = up_down_parts(up_at, up_all, cotangent)
     low_up = lax.psum(up_part, ("tensor", "sub")).astype(jnp.float32)
     low_up = (adapter_scale * low_up).astype(jnp.bfloat16)
     terms = summed_terms(order, slot, low_up, tokens, 1.0)
-    weight = lax.all_gather(frozen_weight, "adapter", axis=1, tiled=True)
-    frozen_product = jnp.dot(tokens, weight, preferred_element_type=jnp.float32)
+
+    frozen_weight, up_all = lax.optimization_barrier((frozen_weight, up_all))
+    weights, weight_place = from_owners(frozen_weight, owners)
+    frozen_part = jnp.dot(
+        tokens, jnp.concatenate(weights, axis=1), preferred_element_type=jnp.float32
+    )
+    frozen_sum = lax.psum_scatter(
+        frozen_part.astype(jnp.bfloat16), ("tensor", "sub"), scatter_dimension=0, tiled=True
+    )
+    lanes = lax.axis_size("tensor") * lax.axis_size("sub")
+    up_blocks = jnp.take(up_all, up_at, axis=0, mode="clip")
+    up_wide = lax.all_to_all(
+        up_blocks, ("tensor", "sub"), split_axis=0, concat_axis=2, tiled=True
+    )
+
+    def line_tracks(w):
+        base = jnp.stack([
+            jnp.stack([w[0, 0] * 0, w[0, 3] + w[0, 2], w[0, 3], w[0, 0] * 0]),
+            jnp.stack([w[0, 3] + w[0, 2], w[0, 0] * 0, w[0, 3] + w[0, 2] + w[1, 3], w[0, 3] + w[0, 2]]),
+            jnp.stack([w[0, 3], w[0, 3] + w[0, 2] + w[1, 3], w[0, 0] * 0, w[0, 3]]),
+            jnp.stack([w[0, 0] * 0, w[0, 3] + w[0, 2], w[0, 3], w[0, 0] * 0]),
+        ])
+        row = lax.dynamic_index_in_dim(base, me, 0, False)
+        jumps = (me + jnp.arange(owners) == 5)[:, None]
+
+        def track(k):
+            return row[:, None] + k + jnp.where(jumps & (k >= w[0, 2]), w[1, 3], 0)
+
+        return track
+
+    def line(index, tracks, tables, terms, tokens):
+        track = line_tracks(count + count.T)
+        t = jnp.arange(tracks)
+        peer = jnp.arange(owners)
+        table_track = track(rank_of)
+        term_track = track(count_of[:, None] + rank_in)
+        takes_table = mine_of[:, :, None] * i32(table_track[:, :, None] == t)
+        takes_term = mine_in[:, :, None] * i32(term_track[:, :, None] == t)
+        ways = jnp.stack([peer > me, peer < me])[:, :, None, None]
+        takes_table = ways * takes_table
+        takes_term = ways * takes_term
+        table_at = jnp.sum(takes_table * jnp.arange(reg_dev)[:, None], axis=(1, 2)).reshape(-1)
+        term_at = jnp.sum(takes_term * term_slot[:, :, None], axis=(1, 2)).reshape(-1)
+        has_table = jnp.sum(takes_table, axis=(1, 2)).reshape(-1)
+        has_term = jnp.sum(takes_term, axis=(1, 2)).reshape(-1)
+        kind = i32(jnp.where(has_table > 0, 0, jnp.where(has_term > 0, 1, 2)))
+        send = pack(table_at, term_at, kind, tables, terms)
+        parts = 2
+        mask = jnp.repeat(i32(kind < 2), parts)
+        got = line_exchange(
+            tracks * parts, index, send.reshape(2 * tracks * parts, rank_width // parts, d_part), mask
+        ).reshape(2 * tracks, rank_width, d_part)
+        side = jnp.where(peer < me, 0, tracks)[:, None]
+        flat = (side + track(rank_in)).reshape(-1)
+        own = i32(block_owner[:, 0] == me)
+        got_at = jnp.sum(i32(region[:, None] == jnp.arange(regions)) * flat, axis=1) * (1 - own)
+        inner = inner_parts(got_at, block_region * own, own, got, tables, tokens)
+        remote = mine_of.T * (1 - i32(peer == me))
+        back_at = (side + track(count_in[:, None] + rank_of)).T
+        own_terms = lax.dynamic_index_in_dim(mine_in, me, 0, False)
+        own_slots = lax.dynamic_index_in_dim(term_slot, me, 0, False)
+        valid = jnp.concatenate([remote, own_terms[:, None]], axis=1)
+        grad = owner_sum(back_at * remote, own_slots * own_terms, valid, got, terms, reg_dev)
+        return inner, grad
 
     def exchange(slots, tables, terms, tokens):
         s = jnp.arange(slots)
@@ -293,27 +471,43 @@
         grad = owner_sum(back_at * remote, own_slots * own_terms, valid, got, terms, reg_dev)
         return inner, grad
 
-    full = 2 * slot_limit
-    sizes = sorted({-(-full * f // 16) for f in (8, 9, 10, 11, 12, 14, 16)})
+    if owners == 4:
+        both = counts + jnp.swapaxes(counts, 1, 2)
+        ids = jnp.arange(owners)
+        loads = []
+        for cut in range(owners - 1):
+            over = i32((ids[:, None] <= cut) & (ids[None, :] > cut))
+            loads.append(jnp.max(jnp.sum(both * over, axis=(1, 2))))
+        need = jnp.max(jnp.stack(loads))
+        full = blocks * owners
+        sizes = sorted({-(-full * f // 64) for f in (26, 28, 30, 32, 38, 64)})
+        bodies = [functools.partial(line, i, n) for i, n in enumerate(sizes)]
+    else:
+        full = 2 * slot_limit
+        sizes = sorted({-(-full * f // 16) for f in (8, 10, 12, 16)})
+        bodies = [functools.partial(exchange, n) for n in sizes]
     branch = jnp.sum(i32(need > jnp.array(sizes[:-1], jnp.int32)))
-    inner, grad_down = lax.switch(
-        branch, [functools.partial(exchange, n) for n in sizes], tables, terms, tokens
-    )
+    inner, grad_down = lax.switch(branch, bodies, tables, terms, tokens)
 
     low_down = lax.psum(inner, ("tensor", "sub"))
-    lora = lora_columns(region, low_down, up_all)
-    column_offset = lane_index * key_portion
-    owned = lax.dynamic_slice_in_dim(frozen_product, column_offset, key_portion, 1) + lora
-    frozen_product = lax.dynamic_update_slice_in_dim(frozen_product, owned, column_offset, 1)
-    projected = lax.psum_scatter(
-        frozen_product.astype(jnp.bfloat16), ("tensor", "sub"), scatter_dimension=0, tiled=True
-    )
+    mine = tok_rows // lanes
+    low_mine = lax.dynamic_slice_in_dim(low_down, lane_index * mine, mine, 1)
+    low_mine = low_mine.reshape(rank_width, mine // BLOCK, BLOCK)
+    lora = adapter_scale * jnp.einsum(
+        "rbt,brk->btk", low_mine, up_wide, preferred_element_type=jnp.float32
+    )
+    width = frozen_weight.shape[1]
+    frozen_sum = jnp.concatenate(
+        [lax.dynamic_slice_in_dim(frozen_sum, weight_place[o] * width, width, 1) for o in range(owners)],
+        axis=1,
+    )
+    projected = (frozen_sum.astype(jnp.float32) + lora.reshape(frozen_sum.shape)).astype(jnp.bfloat16)
 
     up_terms = summed_terms(order, slot, low_down, cotangent, adapter_scale)
     s = jnp.arange(slot_limit)
     takes = mine_in[:, :, None] * i32(rank_in[:, :, None] == s)
-    up_at = jnp.sum(takes * term_slot[:, :, None], axis=1).reshape(-1)
-    up_send = jnp.take(up_terms, up_at, axis=0, mode="clip")
+    term_at = jnp.sum(takes * term_slot[:, :, None], axis=1).reshape(-1)
+    up_send = jnp.take(up_terms, term_at, axis=0, mode="clip")
     up_got = lax.all_to_all(
         up_send.reshape(owners, slot_limit, rank_width, key_portion),
         "adapter", split_axis=0, concat_axis=0, tiled=True,

time: 623 us -> 459 us (0.74)
  waiting for transfers between devices: 467 us -> 63.8 us
  Pallas kernels: 72.7 us -> 261 us
  blocking collectives: 13 us -> 43.8 us
    all_to_all x1, waiting for transfers between devices: 272 us -> 0.01 us  [shards(): lax.all_to_all(up_blocks, ('tensor', 'sub'), split_axis=0, concat_axis=2,...]
    pallas_call x1, Pallas kernels: 3.85 us -> 181 us  [line_exchange(): pl.pallas_call(kernel, in_specs=[pl.BlockSpec(memory_space=pl.ANY), pl.Bl...]
    all_gather x2 -> x0, waiting for transfers between devices: 107 us -> none  [the longest x1 75.6 us: shards(): weight = lax.all_gather(frozen_weight, 'adapter', axis=1, tiled=True)]
    unnamed x1, blocking collectives: 13 us -> 43.8 us
    psum x1, waiting for transfers between devices: 29.5 us -> 10.1 us  [shards(): low_down = lax.psum(inner, ('tensor', 'sub'))]
    pallas_call x1, Pallas kernels: 14.8 us -> 26 us  [pack(): pl.pallas_call(kernel, grid_spec=pltpu.PrefetchScalarGridSpec(num_scalar_...]
    all_to_all x1, waiting for transfers between devices: 25.9 us -> 16.6 us  [shards(): lax.all_to_all(up_send.reshape(owners, slot_limit, rank_width, key_portio...]
    ppermute x0 -> x6, starting transfers between devices: none -> 9.3 us  [from_owners(): parts.append(lax.ppermute(x, 'adapter', ring))]
  transfers between devices with their start and end apart: 7 -> 11, of which waited for: 7 -> 4; matrix products, arithmetic and copies ran while one was open for 1% -> 9% of each run, Pallas kernels for 2% -> 57%
where the time goes in v2:
time: 459 us; the launch traced here: 456 us
  Pallas kernels  261 us (57%)
  waiting for transfers between devices  63.8 us (14%)
  blocking collectives  43.8 us (10%)
  between operations  19.9 us (4%)
  local copies, waits for them, and re-layouts  18.6 us (4%)
  starting transfers between devices  17.5 us (4%)
  matrix products  16.6 us (4%)
  other arithmetic  12.3 us (3%)
    pallas_call x1, Pallas kernels, line_exchange(): pl.pallas_call(kernel, in_specs=[pl.BlockSpec(memory_space=pl.ANY), pl.Bl...  181 us
    unnamed x1, blocking collectives  43.8 us
    psum x1, waiting for transfers between devices, shards(): low_up = lax.psum(up_part, ('tensor', 'sub')).astype(jnp.float32)  31 us
    pallas_call x1, Pallas kernels, pack(): pl.pallas_call(kernel, grid_spec=pltpu.PrefetchScalarGridSpec(num_scalar_...  26 us
    pallas_call x2, Pallas kernels, owner_sum(): pl.pallas_call(kernel, grid_spec=pltpu.PrefetchScalarGridSpec(num_scalar_...  18.1 us
    all_to_all x1, waiting for transfers between devices, shards(): lax.all_to_all(up_send.reshape(owners, slot_limit, rank_width, key_portio...  16.6 us
    pallas_call x2, Pallas kernels, summed_terms(): pl.pallas_call(kernel, grid_spec=pltpu.PrefetchScalarGridSpec(num_scalar_...  16.5 us
    dot_general x1, matrix products, shards(): jnp.dot(tokens, jnp.concatenate(weights, axis=1), preferred_element_type=...  13.9 us
  transfers between devices with their start and end apart: 11, of which 4 were waited for; matrix products, arithmetic and copies ran while one was open for 9% of the time, Pallas kernels for 57%

profile of v2, /device:TPU:0, one launch (start us, length us, event | category | flops | bytes accessed | tf_op | source)
XLA Modules:
  0.0 455.9 jit_solution(3681100359123276891)
XLA Ops:
  7.2 3.1 collective-permute-start
  10.3 2.6 collective-permute-start.1
  12.9 1.3 collective-permute-start.2
  14.3 1.2 dynamic-slice.8
  17.7 43.8 %all-reduce.1 = s32[128]{0:T(128)S(1)} all-reduce(s32[128]{0:T(128)S(1)} %get-tuple-element.762), channel_id=1, replica_groups=mesh['groups'=2,'adapter'=4,'tensor'=2,'sub'=2] {'groups','adapter'}, use_global_device_ids=true, to_apply=%add.1 | all-reduce | flops 128 | bytes 1024
  66.5 1.3 fusion.74
  69.3 1.6 collective-permute-start.5
  71.7 6.8 %shard_map.103 = bf16[64,2048]{1,0:T(8,128)(2,1)} custom-call(s32[16]{0:T(128)S(1)} %get-tuple-element.850.region_ref, bf16[64,64,256]{2,1,0:T(8,128)(2,1)S(1)} %constant_dynamic-update-slice_fusion.up_ref, bf16[2048,256]{1,0:T(8,128)(2,1)S(1)} %copy-done.5), custom_call_target="tpu_custom_call" | custom-call | tf_op jit(solution)/shard_map/pallas_call | solution.py:35
  78.5 1.3 copy-done.4
  81.0 31.0 %all-reduce.5.cloned.1.call-done = bf16[64,2048]{1,0:T(8,128)(2,1)} async-done(((bf16[64,2048]{1,0:T(8,128)(2,1)}), bf16[64,2048]{1,0:T(8,128)(2,1)}) %all-reduce.5.cloned.1.call-update) | async-done | bytes 262160 | tf_op jit(solution)/shard_map/psum | solution.py:375
  113.0 13.3 %shard_map.104 = bf16[16,64,2048]{2,1,0:T(8,128)(2,1)} custom-call(s32[16]{0:T(128)S(1)} %get-tuple-element.735.order_ref, s32[16]{0:T(128)S(1)} %get-tuple-element.734.slot_ref, bf16[64,2048]{1,0:T(8,128)(2,1)S(1)} %multiply_convert_fusion.low_ref, bf16[2048,2048]{1,0:T(8,128)(2,1)} %val_ref.2), custom_call_target="tpu_custom_call" | custom-call | tf_op jit(solution)/shard_map/pallas_call | solution.py:71
  126.3 240.7 %conditional.1 = (bf16[64,2048]{1,0:T(8,128)(2,1)S(1)}, bf16[16,64,2048]{2,1,0:T(8,128)(2,1)}) conditional(s32[]{:T(128)} %clamp.31, (s32[16]{0:T(128)S(1)}, s32[]{:T(128)}, s32[4,4]{1,0:T(4,128)S(1)}, s32[4,16]{1,0:T(4,128)S(1)}, s32[16,1]{0,1:T(1,128)S(1)}, /*index=5*/s32[16]{0:T(128)S(1)}, s32[4,16]{1,0:T(4,128)S(1)}, ...), branch_computations={%region_18.24_spmd, %region_24.30_spmd, %region_30.36_spmd, %regio... | conditional | flops 87229 | bytes 234922768 | solution.py:490
  130.8 1.3 select_add_fusion.2
  133.2 26.0 %branch_1_fun.4 = bf16[56,64,2048]{2,1,0:T(8,128)(2,1)} custom-call(s32[56]{0:T(128)S(1)} %reshape.740.table_ref_at, s32[56]{0:T(128)S(1)} %reshape.741.term_ref_at, s32[56]{0:T(128)S(1)} %select_n.203.kind_ref, bf16[16,64,2048]{2,1,0:T(8,128)(2,1)} %get-tuple-element.219.table_ref, bf16[16,64,2048]{2,1,0:T(8,128)(2,1)} %get-tuple-element.220.term_ref.refs_4_), custom_call_target="tpu_custom_call" | custom-call | tf_op jit(solution)/shard_map/cond/branch_1_fun/pallas_call | solution.py:103
  159.4 181.1 %branch_1_fun.5 = bf16[112,32,2048]{2,1,0:T(8,128)(2,1)} custom-call(bf16[112,32,2048]{2,1,0:T(8,128)(2,1)} %bitcast.285, s32[112]{0:T(128)S(1)} %reshape.743.mask_ref), custom_call_target="tpu_custom_call" | custom-call | tf_op jit(solution)/shard_map/cond/branch_1_fun/pallas_call | solution.py:292
  340.5 12.8 %branch_1_fun.6 = bf16[64,2048]{1,0:T(8,128)(2,1)S(1)} custom-call(s32[16]{0:T(128)S(1)} %get-tuple-element.744.got_ref_at, s32[16]{0:T(128)S(1)} %get-tuple-element.785.own_ref_at, s32[16]{0:T(128)S(1)} %get-tuple-element.745.own_ref, bf16[56,64,2048]{2,1,0:T(8,128)(2,1)} %bitcast.276, bf16[16,64,2048]{2,1,0:T(8,128)(2,1)S(1)} %copy-done.15, ...), custom_call_target="tpu_custom_call" | custom-call | tf_op jit(solution)/shard_map/cond/branch_1_fun/pallas_call | solution.py:134
  353.4 1.3 bitcast_multiply_fusion.1
  354.9 12.1 %branch_1_fun.7 = bf16[16,64,2048]{2,1,0:T(8,128)(2,1)} custom-call(s32[16,4]{1,0:T(8,128)S(1)} %get-tuple-element.742.got_ref_at, s32[16]{0:T(128)S(1)} %get-tuple-element.780.own_ref_at, s32[16,5]{1,0:T(8,128)S(1)} %pad_add_fusion.2.valid_ref, bf16[56,64,2048]{2,1,0:T(8,128)(2,1)} %bitcast.277, bf16[56,64,2048]{2,1,0:T(8,128)(2,1)} %bitcast.278, ...), custom_call_target="tpu_custom_call" | custom-call | tf_op jit(solution)/shard_map/cond/branch_1_fun/pallas_call | solution.py:170
  367.8 13.9 %convert_bitcast_fusion = bf16[2048,1024]{0,1:T(8,128)(2,1)} fusion(bf16[2048,2048]{1,0:T(8,128)(2,1)} %val_ref.2, bf16[2048,256]{1,0:T(8,128)(2,1)} %collective-permute-done.5, bf16[2048,256]{1,0:T(8,128)(2,1)} %collective-permute-done.4, bf16[2048,256]{1,0:T(8,128)(2,1)} %collective-permute-done.3, bf16[2048,256]{1,0:T(8,128)(2,1)} %param.15), kind=kOutput, calls=%fused_computation.268 | convolution fusion | flops 8608808960 | bytes 16777216 | tf_op jit(solution)/shard_map/dot_general | solution.py:381
  382.3 3.0 gather_fusion
  385.3 3.5 all-to-all-start
  389.0 10.1 %all-reduce.7.cloned.1.call-done.low_ref = bf16[64,2048]{1,0:T(8,128)(2,1)} async-done(((bf16[64,2048]{1,0:T(8,128)(2,1)}), bf16[64,2048]{1,0:T(8,128)(2,1)}) %all-reduce.7.cloned.1.call-update) | async-done | bytes 262160 | tf_op jit(solution)/shard_map/psum | solution.py:492
  400.0 3.2 shard_map.105
  403.3 1.6 gather_fusion.1
  404.9 4.6 %all-to-all-start.1 = ((bf16[4,8,64,256]{3,2,1,0:T(8,128)(2,1)}), bf16[4,8,64,256]{3,2,1,0:T(8,128)(2,1)S(1)}, u32[]{:S(2)}, u32[]{:S(2)}) async-start(bf16[4,8,64,256]{3,2,1,0:T(8,128)(2,1)} %bitcast.130), calls=%async_computation.2 | async-start | bytes 2097152 | tf_op jit(solution)/shard_map/all_to_all | solution.py:511
  413.0 2.7 convolution_multiply_fusion
  415.6 1.9 copy.255
  417.6 16.6 %all-to-all-done.1 = bf16[4,8,64,256]{3,2,1,0:T(8,128)(2,1)S(1)} async-done(((bf16[4,8,64,256]{3,2,1,0:T(8,128)(2,1)}), bf16[4,8,64,256]{3,2,1,0:T(8,128)(2,1)S(1)}, u32[]{:S(2)}, u32[]{:S(2)}) %all-to-all-start.1) | async-done | bytes 1048608 | tf_op jit(solution)/shard_map/all_to_all | solution.py:511
  434.2 6.1 %shard_map.106 = bf16[16,64,256]{2,1,0:T(8,128)(2,1)} custom-call(s32[16,4]{1,0:T(8,128)S(1)} %bitcast_multiply_fusion.6.got_ref_at, s32[16]{0:T(128)S(1)} %broadcast_71_own_ref_at.2.own_ref_at, s32[16,5]{1,0:T(8,128)S(1)} %concatenate.57.valid_ref, bf16[32,64,256]{2,1,0:T(8,128)(2,1)S(1)} %bitcast.245, bf16[32,64,256]{2,1,0:T(8,128)(2,1)S(1)} %bitcast.246, ...), custom_call_target="tpu_custom_call" | custom-call | tf_op jit(solution)/shard_map/pallas_call | solution.py:170
  440.3 6.1 %reduce-scatter.2.cloned.1.call-done = bf16[512,1024]{0,1:T(8,128)(2,1)} async-done(((bf16[2048,1024]{0,1:T(8,128)(2,1)}), bf16[512,1024]{0,1:T(8,128)(2,1)}) %reduce-scatter.2.cloned.1.call-update) | async-done | bytes 1048592 | tf_op jit(solution)/shard_map/reduce_scatter | solution.py:384
  446.3 1.3 constant_dynamic-slice_fusion.28
  448.0 1.3 copy.254
  (134 shorter events, 16.1 us)
Async XLA Ops:
  7.2 64.6 %copy-start.5 = (bf16[2048,256]{1,0:T(8,128)(2,1)S(1)}, bf16[2048,256]{1,0:T(8,128)(2,1)}, u32[]{:S(2)}) copy-start(bf16[2048,256]{1,0:T(8,128)(2,1)} %val_ref.3) | copy-start | bytes 3145732
  7.2 104.8 %all-reduce.5.cloned.1.call-start = ((), (), s32[]{:S(2)}) async-start(), calls=%async_computation.4 | async-start | bytes 524288 | tf_op jit(solution)/shard_map/psum | solution.py:375
  7.2 62.0 %collective-permute-start = (bf16[16,64,256]{2,1,0:T(8,128)(2,1)}, bf16[16,64,256]{2,1,0:T(8,128)(2,1)S(1)}, u32[]{:S(2)}, u32[]{:S(2)}) collective-permute-start(bf16[16,64,256]{2,1,0:T(8,128)(2,1)} %param.17), channel_id=1, source_target_pairs={{0,4},{4,8},{8,12},{12,0},{1,5},{5,9},{9,13},{13,1},{2,6},{6,10},{... | collective-permute-start | bytes 1572872 | tf_op jit(solution)/shard_map/ppermute | solution.py:321
  10.3 58.9 %collective-permute-start.1 = (bf16[16,64,256]{2,1,0:T(8,128)(2,1)}, bf16[16,64,256]{2,1,0:T(8,128)(2,1)S(1)}, u32[]{:S(2)}, u32[]{:S(2)}) collective-permute-start(bf16[16,64,256]{2,1,0:T(8,128)(2,1)} %param.17), channel_id=1, source_target_pairs={{0,8},{4,12},{8,0},{12,4},{1,9},{5,13},{9,1},{13,5},{2,10},{6,14},... | collective-permute-start | bytes 1572872 | tf_op jit(solution)/shard_map/ppermute | solution.py:321
  12.9 56.4 %collective-permute-start.2 = (bf16[16,64,256]{2,1,0:T(8,128)(2,1)}, bf16[16,64,256]{2,1,0:T(8,128)(2,1)S(1)}, u32[]{:S(2)}, u32[]{:S(2)}) collective-permute-start(bf16[16,64,256]{2,1,0:T(8,128)(2,1)} %param.17), channel_id=1, source_target_pairs={{0,12},{4,0},{8,4},{12,8},{1,13},{5,1},{9,5},{13,9},{2,14},{6,2},{... | collective-permute-start | bytes 1572872 | tf_op jit(solution)/shard_map/ppermute | solution.py:321
  14.3 2.6 copy-start.23
  17.7 95.2 %copy-start.12 = (s32[16]{0:T(128)}, s32[16]{0:T(128)S(1)}, u32[]{:S(2)}) copy-start(s32[16]{0:T(128)S(1)} %get-tuple-element.850.region_ref) | copy-start | bytes 196
  69.3 298.4 %collective-permute-start.5 = (bf16[2048,256]{1,0:T(8,128)(2,1)}, bf16[2048,256]{1,0:T(8,128)(2,1)}, u32[]{:S(2)}, u32[]{:S(2)}) collective-permute-start(bf16[2048,256]{1,0:T(8,128)(2,1)} %param.15), channel_id=1, source_target_pairs={{0,12},{4,0},{8,4},{12,8},{1,13},{5,1},{9,5},{13,9},{2,14},{6,2},{... | collective-permute-start | bytes 3145736 | tf_op jit(solution)/shard_map/ppermute | solution.py:321
  71.0 296.8 %collective-permute-start.4 = (bf16[2048,256]{1,0:T(8,128)(2,1)}, bf16[2048,256]{1,0:T(8,128)(2,1)}, u32[]{:S(2)}, u32[]{:S(2)}) collective-permute-start(bf16[2048,256]{1,0:T(8,128)(2,1)} %param.15), channel_id=1, source_target_pairs={{0,8},{4,12},{8,0},{12,4},{1,9},{5,13},{9,1},{13,5},{2,10},{6,14},... | collective-permute-start | bytes 3145736 | tf_op jit(solution)/shard_map/ppermute | solution.py:321
  71.0 296.8 %collective-permute-start.3 = (bf16[2048,256]{1,0:T(8,128)(2,1)}, bf16[2048,256]{1,0:T(8,128)(2,1)}, u32[]{:S(2)}, u32[]{:S(2)}) collective-permute-start(bf16[2048,256]{1,0:T(8,128)(2,1)} %param.15), channel_id=1, source_target_pairs={{0,4},{4,8},{8,12},{12,0},{1,5},{5,9},{9,13},{13,1},{2,6},{6,10},{... | collective-permute-start | bytes 3145736 | tf_op jit(solution)/shard_map/ppermute | solution.py:321
  78.5 1.4 copy-start.4
  79.9 319.2 %all-reduce.7.cloned.1.call-start = ((), (), s32[]{:S(2)}) async-start(), calls=%async_computation.5 | async-start | bytes 524288 | tf_op jit(solution)/shard_map/psum | solution.py:492
  81.0 45.3 %copy-start.8 = (s32[16]{0:T(128)}, s32[16]{0:T(128)S(1)}, u32[]{:S(2)}) copy-start(s32[16]{0:T(128)S(1)} %get-tuple-element.734.slot_ref) | copy-start | bytes 196
  81.0 45.3 %copy-start.10 = (s32[16]{0:T(128)}, s32[16]{0:T(128)S(1)}, u32[]{:S(2)}) copy-start(s32[16]{0:T(128)S(1)} %get-tuple-element.735.order_ref) | copy-start | bytes 196
  113.0 13.3 %copy-start.21 = (s32[16]{0:T(128)S(1)}, s32[16]{0:T(128)}, u32[]{:S(2)}) copy-start(s32[16]{0:T(128)} %param.20) | copy-start | bytes 196
  113.0 13.3 %copy-start.22 = (s32[16,1]{0,1:T(1,128)S(1)}, s32[16,1]{0,1:T(1,128)}, u32[]{:S(2)}) copy-start(s32[16,1]{0,1:T(1,128)} %param.19) | copy-start | bytes 196
  159.4 181.1 %copy-start.15 = (bf16[16,64,2048]{2,1,0:T(8,128)(2,1)S(1)}, bf16[16,64,2048]{2,1,0:T(8,128)(2,1)}, u32[]{:S(2)}) copy-start(bf16[16,64,2048]{2,1,0:T(8,128)(2,1)} %get-tuple-element.219.table_ref) | copy-start | bytes 12582916 | tf_op jit(solution)/shard_map/cond
  367.0 0.7 copy-start.20
  367.7 78.6 %reduce-scatter.2.cloned.1.call-start = ((), (), s32[]{:S(2)}) async-start(), calls=%async_computation.3 | async-start | bytes 5242880 | tf_op jit(solution)/shard_map/reduce_scatter | solution.py:384
  381.7 0.6 copy-start.13
  381.7 17.4 %copy-start.6 = (bf16[2048,256]{1,0:T(8,128)(2,1)S(1)}, bf16[2048,256]{1,0:T(8,128)(2,1)}, u32[]{:S(2)}) copy-start(bf16[2048,256]{1,0:T(8,128)(2,1)} %val_ref.3) | copy-start | bytes 3145732
  381.7 17.4 %copy-start.9 = (s32[16]{0:T(128)S(1)}, s32[16]{0:T(128)}, u32[]{:S(2)}) copy-start(s32[16]{0:T(128)} %copy-done.8) | copy-start | bytes 196
  381.7 17.4 %copy-start.11 = (s32[16]{0:T(128)S(1)}, s32[16]{0:T(128)}, u32[]{:S(2)}) copy-start(s32[16]{0:T(128)} %copy-done.10) | copy-start | bytes 196
  382.3 27.2 %copy-start.24 = (s32[4]{0:T(128)S(1)}, s32[4]{0:T(128)}, u32[]{:S(2)}) copy-start(s32[4]{0:T(128)} %copy-done.23) | copy-start | bytes 52
  385.3 19.6 %all-to-all-start = ((bf16[16,64,256]{2,1,0:T(8,128)(2,1)}), bf16[16,64,256]{2,1,0:T(8,128)(2,1)S(1)}, u32[]{:S(2)}, u32[]{:S(2)}) async-start(bf16[16,64,256]{2,1,0:T(8,128)(2,1)} %gather_fusion), calls=%async_computation.1 | async-start | bytes 1048576 | tf_op jit(solution)/shard_map/all_to_all | solution.py:389
  399.1 1.0 copy-start.7
  404.9 29.3 %all-to-all-start.1 = ((bf16[4,8,64,256]{3,2,1,0:T(8,128)(2,1)}), bf16[4,8,64,256]{3,2,1,0:T(8,128)(2,1)S(1)}, u32[]{:S(2)}, u32[]{:S(2)}) async-start(bf16[4,8,64,256]{3,2,1,0:T(8,128)(2,1)} %bitcast.130), calls=%async_computation.2 | async-start | bytes 2097152 | tf_op jit(solution)/shard_map/all_to_all | solution.py:511
Sparse Core Ops, SparseCore 0:
  80.0 31.8 all-reduce.4
  367.8 31.1 all-reduce.6
  401.6 44.6 reduce-scatter.1

commit v3 on v2

--- a/solution.py
+++ b/solution.py
@@ -89,29 +89,38 @@
     count = kind.shape[0]
     _, rank, cols = tables.shape
 
-    def kernel(table_ref_at, term_ref_at, kind_ref, table_ref, term_ref, out_ref):
-        what = kind_ref[pl.program_id(0)]
-
-        @pl.when(what == 0)
-        def _():
-            out_ref[...] = table_ref[...]
-
-        @pl.when(what == 1)
-        def _():
-            out_ref[...] = term_ref[...]
-
+    def kernel(table_ref_at, term_ref_at, kind_ref, table_ref, term_ref, out_ref, sem):
+        def start(i, carry):
+            what = kind_ref[i]
+
+            @pl.when(what == 0)
+            def _():
+                pltpu.make_async_copy(table_ref.at[table_ref_at[i]], out_ref.at[i], sem.at[i]).start()
+
+            @pl.when(what == 1)
+            def _():
+                pltpu.make_async_copy(term_ref.at[term_ref_at[i]], out_ref.at[i], sem.at[i]).start()
+
+            return carry
+
+        def finish(i, carry):
+            @pl.when(kind_ref[i] < 2)
+            def _():
+                pltpu.make_async_copy(table_ref.at[0], out_ref.at[i], sem.at[i]).wait()
+
+            return carry
+
+        lax.fori_loop(0, count, start, 0)
+        lax.fori_loop(0, count, finish, 0)
+
+    smem = pl.BlockSpec(memory_space=pltpu.SMEM)
+    hbm = pl.BlockSpec(memory_space=pl.ANY)
     return pl.pallas_call(
         kernel,
-        grid_spec=pltpu.PrefetchScalarGridSpec(
-            num_scalar_prefetch=3,
-            grid=(count,),
-            in_specs=[
-                pl.BlockSpec((1, rank, cols), lambda i, a, b, k: (a[i], 0, 0)),
-                pl.BlockSpec((1, rank, cols), lambda i, a, b, k: (b[i], 0, 0)),
-            ],
-            out_specs=pl.BlockSpec((1, rank, cols), lambda i, a, b, k: (i, 0, 0)),
-        ),
+        in_specs=[smem, smem, smem, hbm, hbm],
+        out_specs=hbm,
         out_shape=jax.ShapeDtypeStruct((count, rank, cols), tables.dtype),
+        scratch_shapes=[pltpu.SemaphoreType.DMA((count,))],
         compiler_params=params(),
     )(table_at, term_at, kind, tables, terms)
 
@@ -339,9 +348,25 @@
     tables = jnp.swapaxes(down_tables, 1, 2)
 
     region = block_owner[:, 0] * reg_dev + block_region
-    named = lax.all_gather(region, ("groups", "adapter"), axis=0, tiled=True)
+    j = jnp.arange(blocks)
+    less = region[:, None] < region[None, :]
+    tie = (region[:, None] == region[None, :]) & (j[:, None] < j[None, :])
+    place = jnp.sum(i32(less | tie), axis=0)
+    order = jnp.sum(i32(place[:, None] == j[None, :]) * j[:, None], axis=0)
+    first = jnp.sum(i32(less), axis=0)
+    slot = jnp.sum(i32(place[:, None] == j[None, :]) * first[:, None], axis=0)
+    regions = owners * reg_dev
+    term_slot = jnp.sum(i32(region[:, None] < jnp.arange(regions)[None, :]), axis=0)
+    term_slot = jnp.minimum(term_slot, blocks - 1).reshape(owners, reg_dev)
+
+    up_parts, up_place = from_owners(up_tables, owners)
+    up_all = jnp.concatenate(up_parts, axis=0)
+    up_at = jnp.sum(i32(block_owner == jnp.arange(owners)) * up_place, axis=1) * reg_dev + block_region
+    up_part = up_down_parts(up_at, up_all, cotangent)
+    up_part, late_region = lax.optimization_barrier((up_part, region))
+
+    named = lax.all_gather(late_region, ("groups", "adapter"), axis=0, tiled=True)
     named = named.reshape(-1, owners, blocks)
-    regions = owners * reg_dev
     present = i32(jnp.any(named[..., None] == jnp.arange(regions), axis=2))
     present = present.reshape(-1, owners, owners, reg_dev)
     counts = jnp.sum(present, axis=-1)
@@ -358,37 +383,23 @@
     count_in = lax.dynamic_index_in_dim(count, me, 0, False)
     count_of = lax.dynamic_index_in_dim(count, me, 1, False)
 
-    j = jnp.arange(blocks)
-    less = region[:, None] < region[None, :]
-    tie = (region[:, None] == region[None, :]) & (j[:, None] < j[None, :])
-    place = jnp.sum(i32(less | tie), axis=0)
-    order = jnp.sum(i32(place[:, None] == j[None, :]) * j[:, None], axis=0)
-    first = jnp.sum(i32(less), axis=0)
-    slot = jnp.sum(i32(place[:, None] == j[None, :]) * first[:, None], axis=0)
-    term_slot = jnp.sum(i32(region[:, None] < jnp.arange(regions)[None, :]), axis=0)
-    term_slot = jnp.minimum(term_slot, blocks - 1).reshape(owners, reg_dev)
-
-    up_parts, up_place = from_owners(up_tables, owners)
-    up_all = jnp.concatenate(up_parts, axis=0)
-    up_at = jnp.sum(i32(block_owner == jnp.arange(owners)) * up_place, axis=1) * reg_dev + block_region
-    up_part = up_down_parts(up_at, up_all, cotangent)
     low_up = lax.psum(up_part, ("tensor", "sub")).astype(jnp.float32)
     low_up = (adapter_scale * low_up).astype(jnp.bfloat16)
     terms = summed_terms(order, slot, low_up, tokens, 1.0)
 
     frozen_weight, up_all = lax.optimization_barrier((frozen_weight, up_all))
     weights, weight_place = from_owners(frozen_weight, owners)
-    frozen_part = jnp.dot(
-        tokens, jnp.concatenate(weights, axis=1), preferred_element_type=jnp.float32
-    )
-    frozen_sum = lax.psum_scatter(
-        frozen_part.astype(jnp.bfloat16), ("tensor", "sub"), scatter_dimension=0, tiled=True
-    )
+    weight = jnp.concatenate(weights, axis=1)
     lanes = lax.axis_size("tensor") * lax.axis_size("sub")
     up_blocks = jnp.take(up_all, up_at, axis=0, mode="clip")
     up_wide = lax.all_to_all(
         up_blocks, ("tensor", "sub"), split_axis=0, concat_axis=2, tiled=True
     )
+
+    def finish(inner, tokens, weight):
+        low_down = lax.psum(inner, ("tensor", "sub"))
+        frozen = jnp.dot(tokens, weight, preferred_element_type=jnp.float32)
+        return low_down, frozen.astype(jnp.bfloat16)
 
     def line_tracks(w):
         base = jnp.stack([
@@ -405,7 +416,7 @@
 
         return track
 
-    def line(index, tracks, tables, terms, tokens):
+    def line(index, tracks, tables, terms, tokens, weight):
         track = line_tracks(count + count.T)
         t = jnp.arange(tracks)
         peer = jnp.arange(owners)
@@ -438,9 +449,9 @@
         own_slots = lax.dynamic_index_in_dim(term_slot, me, 0, False)
         valid = jnp.concatenate([remote, own_terms[:, None]], axis=1)
         grad = owner_sum(back_at * remote, own_slots * own_terms, valid, got, terms, reg_dev)
-        return inner, grad
-
-    def exchange(slots, tables, terms, tokens):
+        return finish(inner, tokens, weight), grad
+
+    def exchange(slots, tables, terms, tokens, weight):
         s = jnp.arange(slots)
         takes_table = mine_of[:, :, None] * i32(rank_of[:, :, None] == s)
         shifted = rank_in + count_of[:, None]
@@ -469,7 +480,7 @@
         own_slots = lax.dynamic_index_in_dim(term_slot, me, 0, False)
         valid = jnp.concatenate([remote, own_terms[:, None]], axis=1)
         grad = owner_sum(back_at * remote, own_slots * own_terms, valid, got, terms, reg_dev)
-        return inner, grad
+        return finish(inner, tokens, weight), grad
 
     if owners == 4:
         both = counts + jnp.swapaxes(counts, 1, 2)
@@ -480,16 +491,18 @@
             loads.append(jnp.max(jnp.sum(both * over, axis=(1, 2))))
         need = jnp.max(jnp.stack(loads))
         full = blocks * owners
-        sizes = sorted({-(-full * f // 64) for f in (26, 28, 30, 32, 38, 64)})
+        sizes = sorted({-(-full * f // 64) for f in (26, 27, 28, 29, 30, 32, 36, 64)})
         bodies = [functools.partial(line, i, n) for i, n in enumerate(sizes)]
     else:
         full = 2 * slot_limit
         sizes = sorted({-(-full * f // 16) for f in (8, 10, 12, 16)})
         bodies = [functools.partial(exchange, n) for n in sizes]
     branch = jnp.sum(i32(need > jnp.array(sizes[:-1], jnp.int32)))
-    inner, grad_down = lax.switch(branch, bodies, tables, terms, tokens)
-
-    low_down = lax.psum(inner, ("tensor", "sub"))
+    (low_down, frozen_part), grad_down = lax.switch(branch, bodies, tables, terms, tokens, weight)
+
+    frozen_sum = lax.psum_scatter(
+        frozen_part, ("tensor", "sub"), scatter_dimension=0, tiled=True
+    )
     mine = tok_rows // lanes
     low_mine = lax.dynamic_slice_in_dim(low_down, lane_index * mine, mine, 1)
     low_mine = low_mine.reshape(rank_width, mine // BLOCK, BLOCK)

time: 459 us -> 717 us (1.56)
  Pallas kernels: 261 us -> 490 us
  waiting for transfers between devices: 63.8 us -> 120 us
  blocking collectives: 43.8 us -> 20.2 us
    pallas_call x1, Pallas kernels: 26 us -> 233 us  [pack(): pl.pallas_call(kernel, in_specs=[smem, smem, smem, hbm, hbm], out_specs=h...]
    ppermute x6, waiting for transfers between devices: 0.02 us -> 63.7 us  [from_owners(): parts.append(lax.ppermute(x, 'adapter', ring))]
    unnamed x1, blocking collectives: 43.8 us -> 20.2 us
    pallas_call x1, Pallas kernels: 181 us -> 202 us  [line_exchange(): pl.pallas_call(kernel, in_specs=[pl.BlockSpec(memory_space=pl.ANY), pl.Bl...]
    psum x1, waiting for transfers between devices: 10.1 us -> 1.86 us  [finish(): low_down = lax.psum(inner, ('tensor', 'sub'))]
  transfers between devices with their start and end apart: 11 -> 11, of which waited for: 4 -> 7; matrix products, arithmetic and copies ran while one was open for 9% -> 4% of each run, Pallas kernels for 57% -> 5%
where the time goes in v3:
time: 717 us; the launch traced here: 718 us
  Pallas kernels  490 us (68%)
  waiting for transfers between devices  120 us (17%)
  blocking collectives  20.2 us (3%)
  between operations  19.9 us (3%)
  starting transfers between devices  18.7 us (3%)
  other arithmetic  17.3 us (2%)
  matrix products  15.7 us (2%)
  local copies, waits for them, and re-layouts  14.1 us (2%)
    pallas_call x1, Pallas kernels, pack(): pl.pallas_call(kernel, in_specs=[smem, smem, smem, hbm, hbm], out_specs=h...  233 us
    pallas_call x1, Pallas kernels, line_exchange(): pl.pallas_call(kernel, in_specs=[pl.BlockSpec(memory_space=pl.ANY), pl.Bl...  202 us
    ppermute x6, waiting for transfers between devices, from_owners(): parts.append(lax.ppermute(x, 'adapter', ring))  63.7 us
    psum x1, waiting for transfers between devices, shards(): low_up = lax.psum(up_part, ('tensor', 'sub')).astype(jnp.float32)  29.2 us
    unnamed x1, blocking collectives  20.2 us
    all_to_all x1, waiting for transfers between devices, shards(): lax.all_to_all(up_send.reshape(owners, slot_limit, rank_width, key_portio...  20.1 us
    pallas_call x2, Pallas kernels, owner_sum(): pl.pallas_call(kernel, grid_spec=pltpu.PrefetchScalarGridSpec(num_scalar_...  19.6 us
    pallas_call x2, Pallas kernels, summed_terms(): pl.pallas_call(kernel, grid_spec=pltpu.PrefetchScalarGridSpec(num_scalar_...  16.5 us
  transfers between devices with their start and end apart: 11, of which 7 were waited for; matrix products, arithmetic and copies ran while one was open for 4% of the time, Pallas kernels for 5%

profile of v3, /device:TPU:0, one launch (start us, length us, event | category | flops | bytes accessed | tf_op | source)
XLA Modules:
  0.0 717.6 jit_solution(9386131351183458953)
XLA Ops:
  7.2 3.1 collective-permute-start
  10.3 2.6 collective-permute-start.1
  12.9 1.3 collective-permute-start.2
  17.9 1.2 dynamic-slice.8
  19.9 5.6 collective-permute-done
  26.6 20.6 %collective-permute-done.1 = bf16[16,64,256]{2,1,0:T(8,128)(2,1)} collective-permute-done((bf16[16,64,256]{2,1,0:T(8,128)(2,1)}, bf16[16,64,256]{2,1,0:T(8,128)(2,1)}, u32[]{:S(2)}, u32[]{:S(2)}) %collective-permute-start.1) | collective-permute-done | bytes 524320 | tf_op jit(solution)/shard_map/ppermute | solution.py:330
  49.4 6.8 shard_map.103
  56.4 20.2 %all-reduce.1 = s32[128]{0:T(128)S(1)} all-reduce(s32[128]{0:T(128)S(1)} %dynamic-update-slice), channel_id=1, replica_groups=mesh['groups'=2,'adapter'=4,'tensor'=2,'sub'=2] {'groups','adapter'}, use_global_device_ids=true, to_apply=%add.1 | all-reduce | flops 128 | bytes 1024
  77.2 1.7 collective-permute-start.5
  78.9 1.8 collective-permute-start.4
  86.5 29.2 %all-reduce.28.cloned.1.call-done = bf16[64,2048]{1,0:T(8,128)(2,1)} async-done(((bf16[64,2048]{1,0:T(8,128)(2,1)}), bf16[64,2048]{1,0:T(8,128)(2,1)}) %all-reduce.28.cloned.1.call-update) | async-done | bytes 262160 | tf_op jit(solution)/shard_map/psum | solution.py:386
  116.7 13.3 %shard_map.104 = bf16[16,64,2048]{2,1,0:T(8,128)(2,1)} custom-call(s32[16]{0:T(128)S(1)} %get-tuple-element.1025.order_ref, s32[16]{0:T(128)S(1)} %get-tuple-element.1024.slot_ref, bf16[64,2048]{1,0:T(8,128)(2,1)S(1)} %multiply_convert_fusion.low_ref, bf16[2048,2048]{1,0:T(8,128)(2,1)} %val_ref.2), custom_call_target="tpu_custom_call" | custom-call | tf_op jit(solution)/shard_map/pallas_call | solution.py:71
  130.0 37.5 %collective-permute-done.4 = bf16[2048,256]{1,0:T(8,128)(2,1)} collective-permute-done((bf16[2048,256]{1,0:T(8,128)(2,1)}, bf16[2048,256]{1,0:T(8,128)(2,1)}, u32[]{:S(2)}, u32[]{:S(2)}) %collective-permute-start.4) | collective-permute-done | bytes 1048608 | tf_op jit(solution)/shard_map/ppermute | solution.py:330
  167.5 3.6 pad_maximum_fusion
  171.1 484.9 %conditional.2 = (bf16[64,2048]{1,0:T(8,128)(2,1)}, bf16[2048,1024]{1,0:T(8,128)(2,1)}, bf16[16,64,2048]{2,1,0:T(8,128)(2,1)}) conditional(s32[]{:T(128)} %clamp.31, (s32[16]{0:T(128)S(1)}, s32[]{:T(128)}, s32[4,4]{1,0:T(4,128)S(1)}, s32[4,16]{1,0:T(4,128)S(1)}, s32[16,1]{0,1:T(1,128)S(1)}, ...), branch_computations={%region_17.24_spmd, %region_24.31_spmd, %region_31.38_spmd, %regio... | conditional | flops 8590153728 | bytes 261662720
  178.3 232.5 %branch_5_fun.4 = bf16[64,64,2048]{2,1,0:T(8,128)(2,1)} custom-call(s32[64]{0:T(128)S(1)} %reshape.938.table_ref_at, s32[64]{0:T(128)S(1)} %reshape.939.term_ref_at, s32[64]{0:T(128)S(1)} %select_n.291.kind_ref, bf16[16,64,2048]{2,1,0:T(8,128)(2,1)} %get-tuple-element.372.table_ref, bf16[16,64,2048]{2,1,0:T(8,128)(2,1)} %get-tuple-element.373.term_ref.refs_4_), custom_call_target="tpu_custom_call" | custom-call | tf_op jit(solution)/shard_map/cond/branch_5_fun/pallas_call | solution.py:118
  410.9 202.4 %branch_5_fun.5 = bf16[128,32,2048]{2,1,0:T(8,128)(2,1)} custom-call(bf16[128,32,2048]{2,1,0:T(8,128)(2,1)} %bitcast.385, s32[128]{0:T(128)S(1)} %reshape.941.mask_ref), custom_call_target="tpu_custom_call" | custom-call | tf_op jit(solution)/shard_map/cond/branch_5_fun/pallas_call | solution.py:301
  613.3 12.0 %branch_5_fun.6 = bf16[64,2048]{1,0:T(8,128)(2,1)} custom-call(s32[16]{0:T(128)S(1)} %get-tuple-element.1050.got_ref_at, s32[16]{0:T(128)S(1)} %get-tuple-element.1133.own_ref_at, s32[16]{0:T(128)S(1)} %get-tuple-element.1051.own_ref, bf16[64,64,2048]{2,1,0:T(8,128)(2,1)} %bitcast.363, bf16[16,64,2048]{2,1,0:T(8,128)(2,1)S(1)} %copy-done.18, ...), custom_call_target="tpu_custom_call" | custom-call | tf_op jit(solution)/shard_map/cond/branch_5_fun/pallas_call | solution.py:143
  625.4 13.8 %fusion.100 = bf16[2048,1024]{1,0:T(8,128)(2,1)} fusion(bf16[2048,2048]{1,0:T(8,128)(2,1)} %get-tuple-element.374.tok_ref, bf16[2048,1024]{1,0:T(8,128)(2,1)} %get-tuple-element.375), kind=kOutput, calls=%fused_computation.433 | convolution fusion | flops 8589934592 | bytes 16777216 | tf_op jit(solution)/shard_map/cond/branch_5_fun/dot_general | solution.py:401
  640.7 13.4 %branch_5_fun.7 = bf16[16,64,2048]{2,1,0:T(8,128)(2,1)} custom-call(s32[16,4]{1,0:T(8,128)S(1)} %get-tuple-element.1048.got_ref_at, s32[16]{0:T(128)S(1)} %get-tuple-element.1128.own_ref_at, s32[16,5]{1,0:T(8,128)S(1)} %pad_add_fusion.10.valid_ref, bf16[64,64,2048]{2,1,0:T(8,128)(2,1)} %bitcast.364, bf16[64,64,2048]{2,1,0:T(8,128)(2,1)} %bitcast.365, ...), custom_call_target="tpu_custom_call" | custom-call | tf_op jit(solution)/shard_map/cond/branch_5_fun/pallas_call | solution.py:179
  654.1 1.9 all-reduce.22.cloned.1.call-done
  657.0 1.4 gather_fusion
  658.4 3.5 all-to-all-start
  661.9 3.2 shard_map.105
  665.1 1.6 gather_fusion.1
  666.7 3.9 all-to-all-done
  670.6 4.6 all-to-all-start.1
  678.8 1.8 convolution_multiply_fusion
  680.7 20.1 %all-to-all-done.1 = bf16[4,8,64,256]{3,2,1,0:T(8,128)(2,1)S(1)} async-done(((bf16[4,8,64,256]{3,2,1,0:T(8,128)(2,1)}), bf16[4,8,64,256]{3,2,1,0:T(8,128)(2,1)S(1)}, u32[]{:S(2)}, u32[]{:S(2)}) %all-to-all-start.1) | async-done | bytes 1048608 | tf_op jit(solution)/shard_map/all_to_all | solution.py:524
  700.8 6.2 shard_map.106
  706.9 1.3 constant_dynamic-slice_fusion.27
  708.2 2.9 fusion.72
  (132 shorter events, 20.3 us)
Async XLA Ops:
  7.2 77.8 %copy-start.27 = (s32[7]{0:T(128)S(1)}, s32[7]{0:T(128)}, u32[]{:S(2)}) copy-start(s32[7]{0:T(128)} %constant.385.clone) | copy-start | bytes 88
  7.2 42.2 %copy-start.8 = (bf16[2048,256]{1,0:T(8,128)(2,1)S(1)}, bf16[2048,256]{1,0:T(8,128)(2,1)}, u32[]{:S(2)}) copy-start(bf16[2048,256]{1,0:T(8,128)(2,1)} %val_ref.3) | copy-start | bytes 3145732
  7.2 108.5 %all-reduce.28.cloned.1.call-start = ((), (), s32[]{:S(2)}) async-start(), calls=%async_computation.11 | async-start | bytes 524288 | tf_op jit(solution)/shard_map/psum | solution.py:386
  7.2 18.3 %collective-permute-start = (bf16[16,64,256]{2,1,0:T(8,128)(2,1)}, bf16[16,64,256]{2,1,0:T(8,128)(2,1)}, u32[]{:S(2)}, u32[]{:S(2)}) collective-permute-start(bf16[16,64,256]{2,1,0:T(8,128)(2,1)} %param.19), channel_id=1, source_target_pairs={{0,4},{4,8},{8,12},{12,0},{1,5},{5,9},{9,13},{13,1},{2,6},{6,10},{... | collective-permute-start | bytes 1572872 | tf_op jit(solution)/shard_map/ppermute | solution.py:330
  10.3 36.9 %collective-permute-start.1 = (bf16[16,64,256]{2,1,0:T(8,128)(2,1)}, bf16[16,64,256]{2,1,0:T(8,128)(2,1)}, u32[]{:S(2)}, u32[]{:S(2)}) collective-permute-start(bf16[16,64,256]{2,1,0:T(8,128)(2,1)} %param.19), channel_id=1, source_target_pairs={{0,8},{4,12},{8,0},{12,4},{1,9},{5,13},{9,1},{13,5},{2,10},{6,14},... | collective-permute-start | bytes 1572872 | tf_op jit(solution)/shard_map/ppermute | solution.py:330
  12.9 35.4 %collective-permute-start.2 = (bf16[16,64,256]{2,1,0:T(8,128)(2,1)}, bf16[16,64,256]{2,1,0:T(8,128)(2,1)}, u32[]{:S(2)}, u32[]{:S(2)}) collective-permute-start(bf16[16,64,256]{2,1,0:T(8,128)(2,1)} %param.19), channel_id=1, source_target_pairs={{0,12},{4,0},{8,4},{12,8},{1,13},{5,1},{9,5},{13,9},{2,14},{6,2},{... | collective-permute-start | bytes 1572872 | tf_op jit(solution)/shard_map/ppermute | solution.py:330
  15.4 0.6 copy-start.25
  17.8 112.2 %copy-start.9 = (s32[16]{0:T(128)}, s32[16]{0:T(128)S(1)}, u32[]{:S(2)}) copy-start(s32[16]{0:T(128)S(1)} %get-tuple-element.1024.slot_ref) | copy-start | bytes 196
  17.8 112.2 %copy-start.11 = (s32[16]{0:T(128)}, s32[16]{0:T(128)S(1)}, u32[]{:S(2)}) copy-start(s32[16]{0:T(128)S(1)} %get-tuple-element.1025.order_ref) | copy-start | bytes 196
  77.2 52.8 %collective-permute-start.5 = (bf16[2048,256]{1,0:T(8,128)(2,1)}, bf16[2048,256]{1,0:T(8,128)(2,1)}, u32[]{:S(2)}, u32[]{:S(2)}) collective-permute-start(bf16[2048,256]{1,0:T(8,128)(2,1)} %param.17), channel_id=1, source_target_pairs={{0,12},{4,0},{8,4},{12,8},{1,13},{5,1},{9,5},{13,9},{2,14},{6,2},{... | collective-permute-start | bytes 3145736 | tf_op jit(solution)/shard_map/ppermute | solution.py:330
  78.9 88.6 %collective-permute-start.4 = (bf16[2048,256]{1,0:T(8,128)(2,1)}, bf16[2048,256]{1,0:T(8,128)(2,1)}, u32[]{:S(2)}, u32[]{:S(2)}) collective-permute-start(bf16[2048,256]{1,0:T(8,128)(2,1)} %param.17), channel_id=1, source_target_pairs={{0,8},{4,12},{8,0},{12,4},{1,9},{5,13},{9,1},{13,5},{2,10},{6,14},... | collective-permute-start | bytes 3145736 | tf_op jit(solution)/shard_map/ppermute | solution.py:330
  80.7 86.8 %collective-permute-start.3 = (bf16[2048,256]{1,0:T(8,128)(2,1)}, bf16[2048,256]{1,0:T(8,128)(2,1)}, u32[]{:S(2)}, u32[]{:S(2)}) collective-permute-start(bf16[2048,256]{1,0:T(8,128)(2,1)} %param.17), channel_id=1, source_target_pairs={{0,4},{4,8},{8,12},{12,0},{1,5},{5,9},{9,13},{13,1},{2,6},{6,10},{... | collective-permute-start | bytes 3145736 | tf_op jit(solution)/shard_map/ppermute | solution.py:330
  116.7 50.9 %copy-start.21 = (bf16[2048,256]{1,0:T(8,128)(2,1)S(1)}, bf16[2048,256]{1,0:T(8,128)(2,1)}, u32[]{:S(2)}) copy-start(bf16[2048,256]{1,0:T(8,128)(2,1)} %param.17) | copy-start | bytes 3145732
  130.0 41.1 %copy-start.23 = (s32[16]{0:T(128)S(1)}, s32[16]{0:T(128)}, u32[]{:S(2)}) copy-start(s32[16]{0:T(128)} %param.22) | copy-start | bytes 196
  130.0 41.1 %copy-start.24 = (s32[16,1]{0,1:T(1,128)S(1)}, s32[16,1]{0,1:T(1,128)}, u32[]{:S(2)}) copy-start(s32[16,1]{0,1:T(1,128)} %param.21) | copy-start | bytes 196
  171.4 484.6 %all-reduce.22.cloned.1.call-start = ((), (), s32[]{:S(2)}) async-start(), calls=%async_computation.8 | async-start | bytes 524288 | tf_op jit(solution)/shard_map/cond/branch_5_fun/psum | solution.py:400
  410.8 202.5 %slice-start.6 = ((s8[8388608]{0:T(1024)(128)(4,1)}), s8[4194304]{0:T(1024)(128)(4,1)S(1)}, s32[]{:S(2)}) async-start(s8[8388608]{0:T(1024)(128)(4,1)} %bitcast.357), calls=%async_computation.19 | async-start | bytes 8388608 | tf_op jit(solution)/shard_map/conditional
  410.8 202.5 %copy-start.18 = (bf16[16,64,2048]{2,1,0:T(8,128)(2,1)S(1)}, bf16[16,64,2048]{2,1,0:T(8,128)(2,1)}, u32[]{:S(2)}) copy-start(bf16[16,64,2048]{2,1,0:T(8,128)(2,1)} %get-tuple-element.372.table_ref) | copy-start | bytes 12582916 | tf_op jit(solution)/shard_map/conditional
  410.8 202.5 %slice-start.7 = ((s8[8388608]{0:T(1024)(128)(4,1)}), s8[4194304]{0:T(1024)(128)(4,1)S(1)}, s32[]{:S(2)}) async-start(s8[8388608]{0:T(1024)(128)(4,1)} %bitcast.357), calls=%async_computation.20 | async-start | bytes 8388608 | tf_op jit(solution)/shard_map/conditional
  656.0 5.9 copy-start.10
  656.0 5.9 copy-start.12
  656.0 5.9 copy-start.22
  656.0 51.0 %reduce-scatter.2.cloned.1.call-start = ((), (), s32[]{:S(2)}) async-start(), calls=%async_computation.12 | async-start | bytes 5242880 | tf_op jit(solution)/shard_map/reduce_scatter | solution.py:503
  656.7 18.5 %copy-start.26 = (s32[4]{0:T(128)S(1)}, s32[4]{0:T(128)}, u32[]{:S(2)}) copy-start(s32[4]{0:T(128)} %copy-done.25) | copy-start | bytes 52
  658.4 12.3 %all-to-all-start = ((bf16[16,64,256]{2,1,0:T(8,128)(2,1)}), bf16[16,64,256]{2,1,0:T(8,128)(2,1)S(1)}, u32[]{:S(2)}, u32[]{:S(2)}) async-start(bf16[16,64,256]{2,1,0:T(8,128)(2,1)} %gather_fusion), calls=%async_computation.1 | async-start | bytes 1048576 | tf_op jit(solution)/shard_map/all_to_all | solution.py:395
  670.6 30.1 %all-to-all-start.1 = ((bf16[4,8,64,256]{3,2,1,0:T(8,128)(2,1)}), bf16[4,8,64,256]{3,2,1,0:T(8,128)(2,1)S(1)}, u32[]{:S(2)}, u32[]{:S(2)}) async-start(bf16[4,8,64,256]{3,2,1,0:T(8,128)(2,1)} %bitcast.165), calls=%async_computation.2 | async-start | bytes 2097152 | tf_op jit(solution)/shard_map/all_to_all | solution.py:524
Sparse Core Ops, SparseCore 0:
  83.2 32.4 all-reduce.27
  625.5 30.4 all-reduce.21
  659.5 44.6 reduce-scatter.1
